TPU v7x, 32 devices: a whole 2x2x4 slice. The times are simulated.
32 devices in a mesh: dp: 4 (over y, core), row: 2 (over x), col: 4 (over z).
Axes of the slice: x: 2, y: 2, z: 4, core: 2. Of those that a mesh axis runs over, the one named last changes fastest.
Arguments:
- block_input: bfloat16 [4096, 2048], P('dp', ('row', 'col')), may hold values from -6 to 6
- segment_ids: int32 [4096], P('dp'), may hold values from 0 to 15, as said below
- positions: int32 [4096], P('dp'), may hold values from 0 to 1278, as said below
- ln_gain: bfloat16 [2048], P(('row', 'col')), may hold values from 0.5 to 1.5
- ln_bias: bfloat16 [2048], P(('row', 'col')), may hold values from -2 to 2
- qkv_weight: bfloat16 [2048, 3, 2048], P('row', None, 'col'), may hold values from -0.125 to 0.125
- qkv_bias: float32 [3, 4, 2, 256], P(None, 'col', 'row'), may hold values from -2 to 2
- dense_weight: bfloat16 [2048, 2048], P('col', 'row'), may hold values from -1.5 to 1.5
- dense_bias: float32 [2048], P(('row', 'col')), may hold values from -2 to 2
- fc1_weight: bfloat16 [2048, 8192], P('row', 'col'), may hold values from -0.125 to 0.125
- fc1_bias: float32 [4, 2, 1024], P('col', 'row'), may hold values from -2 to 2
- fc2_weight: bfloat16 [8192, 2048], P('col', 'row'), may hold values from -0.0625 to 0.0625
- fc2_bias: float32 [2048], P(('row', 'col')), may hold values from -2 to 2
- cotangent: bfloat16 [4096, 2048], P('dp', ('row', 'col')), may hold values from -6 to 6
Outputs:
- block_output: bfloat16 [4096, 2048], P('dp', ('row', 'col'))
- input_grad: float32 [4096, 2048], P('dp', ('row', 'col'))
- ln_gain_grad: float32 [2048], P(('row', 'col'))
- ln_bias_grad: float32 [2048], P(('row', 'col'))
- qkv_weight_grad: float32 [2048, 3, 2048], P('row', None, 'col')
- qkv_bias_grad: float32 [3, 4, 2, 256], P(None, 'col', 'row')
- dense_weight_grad: float32 [2048, 2048], P('col', 'row')
- dense_bias_grad: float32 [2048], P(('row', 'col'))
- fc1_weight_grad: float32 [2048, 8192], P('row', 'col')
- fc1_bias_grad: float32 [4, 2, 1024], P('col', 'row')
- fc2_weight_grad: float32 [8192, 2048], P('col', 'row')
- fc2_bias_grad: float32 [2048], P(('row', 'col'))
Inputs may be any that keep to these rules, and one draw needn't show every extreme that they name: `segment_ids`: each aligned block of 1024 tokens (one index of dp) holds four whole documents end to end, each at least one token; ids never fall, block b holds ids 4 b to 4 b + 3, and one document of every block has exactly 768 tokens. Within a document, positions count up by one from that document's own start offset.
All inputs are finite; a program needn't handle non-finite values.
Results may differ from a plain program's by a relative error of at most 0.0098.
Values may be sent and summed in bfloat16 or wider, within the bound.
A program may use at most 192 MiB of HBM per device.

v0:
```python
import math

import jax
import jax.numpy as jnp
from jax import lax
from jax.sharding import PartitionSpec as P

HEAD_DIM = 64
ROT_DIM = 32
QBLOCK = 512


NORM_EPSILON = 1e-05
MASKED_SCORE = -1e30


def rotary(vectors, positions):
    half_dim = ROT_DIM // 2
    steps_float = jnp.arange(half_dim).astype(jnp.float32)
    frequency = jnp.exp(steps_float * (-2.0 * math.log(10000.0) / ROT_DIM))
    angles = positions.astype(jnp.float32)[:, None] * frequency[None, :]
    cosine = jnp.cos(angles)[:, None, :]
    sine_part = jnp.sin(angles)[:, None, :]
    first_half = vectors[..., :half_dim]
    second_half = vectors[..., half_dim:ROT_DIM]
    rest_dims = vectors[..., ROT_DIM:]
    return jnp.concatenate(
        [
            first_half * cosine - second_half * sine_part,
            second_half * cosine + first_half * sine_part,
            rest_dims,
        ],
        axis=-1,
    )


def block_logits(query_rows, key_rows, row_segs, row_index, segments, key_order):
    raw_scores = jnp.einsum(
        "qhd,khd->hqk", query_rows, key_rows, preferred_element_type=jnp.float32
    )
    allowed = (row_segs[:, None] == segments[None, :]) & (row_index[:, None] >= key_order[None, :])
    return jnp.where(allowed[None], raw_scores * HEAD_DIM ** (-0.5), MASKED_SCORE)


def attend_forward(queries, key_rows, value_rows, segments):
    tokens = queries.shape[0]
    block_rows = min(QBLOCK, tokens)
    block_count = tokens // block_rows
    key_order = jnp.arange(tokens)

    def one_block(block_at):
        first_row = block_at * block_rows
        query_rows = lax.dynamic_slice_in_dim(queries, first_row, block_rows, 0)
        row_segs = lax.dynamic_slice_in_dim(segments, first_row, block_rows, 0)
        row_index = first_row + jnp.arange(block_rows)
        logits = block_logits(query_rows, key_rows, row_segs, row_index, segments, key_order)
        row_top = jnp.max(logits, axis=-1, keepdims=True)
        exponent = jnp.exp(logits - row_top)
        row_total = jnp.sum(exponent, axis=-1, keepdims=True)
        weights = (exponent / row_total).astype(jnp.bfloat16)
        context = jnp.einsum(
            "hqk,khd->qhd", weights, value_rows, preferred_element_type=jnp.float32
        )
        log_total = row_top[..., 0] + jnp.log(row_total[..., 0])
        return (context, log_total)

    contexts, log_totals = lax.map(one_block, jnp.arange(block_count))
    return (contexts.reshape(tokens, -1), log_totals)


def attend_backward(queries, key_rows, value_rows, segments, log_totals, context_grad):
    tokens = queries.shape[0]
    block_rows = min(QBLOCK, tokens)
    block_count = tokens // block_rows
    key_order = jnp.arange(tokens)
    score_scale = HEAD_DIM ** (-0.5)

    def one_block(carry, block_at):
        key_grad, value_grad = carry
        first_row = block_at * block_rows
        query_rows = lax.dynamic_slice_in_dim(queries, first_row, block_rows, 0)
        row_segs = lax.dynamic_slice_in_dim(segments, first_row, block_rows, 0)
        row_index = first_row + jnp.arange(block_rows)
        grad_rows = lax.dynamic_slice_in_dim(context_grad, first_row, block_rows, 0)
        logits = block_logits(query_rows, key_rows, row_segs, row_index, segments, key_order)
        weights = jnp.exp(logits - log_totals[block_at][..., None])
        weight_grad = jnp.einsum(
            "qhd,khd->hqk", grad_rows, value_rows, preferred_element_type=jnp.float32
        )
        centre = jnp.sum(weights * weight_grad, axis=-1, keepdims=True)
        score_grad = (score_scale * weights * (weight_grad - centre)).astype(jnp.bfloat16)
        query_grad = jnp.einsum(
            "hqk,khd->qhd", score_grad, key_rows, preferred_element_type=jnp.float32
        )
        key_grad = key_grad + jnp.einsum(
            "hqk,qhd->khd", score_grad, query_rows, preferred_element_type=jnp.float32
        )
        value_grad = value_grad + jnp.einsum(
            "hqk,qhd->khd",
            weights.astype(jnp.bfloat16),
            grad_rows,
            preferred_element_type=jnp.float32,
        )
        return ((key_grad, value_grad), query_grad)

    zero_grad = jnp.zeros(key_rows.shape, jnp.float32)
    (key_grad, value_grad), query_grads = lax.scan(
        one_block, (zero_grad, zero_grad), jnp.arange(block_count)
    )
    return (query_grads.reshape(key_rows.shape), key_grad, value_grad)


def local(
    block_input,
    segment_ids,
    positions,
    ln_gain,
    ln_bias,
    qkv_weight,
    qkv_bias,
    dense_weight,
    dense_bias,
    fc1_weight,
    fc1_bias,
    fc2_weight,
    fc2_bias,
    cotangent,
):
    n_row = lax.axis_size("row")
    n_col = lax.axis_size("col")
    row_at = lax.axis_index("row")
    col_at = lax.axis_index("col")
    tokens = block_input.shape[0]
    part_width = block_input.shape[1]
    full_width = part_width * n_row * n_col
    row_width = full_width // n_row
    whole_in, gain_full, shift_full = (
        lax.all_gather(block_input, ("row", "col"), axis=1, tiled=True),
        lax.all_gather(ln_gain, ("row", "col"), axis=0, tiled=True),
        lax.all_gather(ln_bias, ("row", "col"), axis=0, tiled=True),
    )
    whole = whole_in.astype(jnp.float32)
    row_mean = jnp.mean(whole, axis=-1, keepdims=True)
    centred = whole - row_mean
    variance = jnp.mean(centred * centred, axis=-1, keepdims=True)
    inv_std = lax.rsqrt(variance + NORM_EPSILON)
    centred_scaled = centred * inv_std
    normed_full = (
        centred_scaled * gain_full.astype(jnp.float32) + shift_full.astype(jnp.float32)
    ).astype(jnp.bfloat16)
    normed_rows = lax.dynamic_slice_in_dim(normed_full, row_at * row_width, row_width, 1)
    part_qkv = jnp.einsum(
        "td,dsk->tsk", normed_rows, qkv_weight, preferred_element_type=jnp.float32
    )
    part_up = jnp.dot(normed_rows, fc1_weight, preferred_element_type=jnp.float32)
    mixed_pre, hidden_pre = (
        lax.psum_scatter(part_qkv, "row", scatter_dimension=2, tiled=True),
        lax.psum_scatter(part_up, "row", scatter_dimension=1, tiled=True),
    )
    mixed_pre = mixed_pre + qkv_bias.reshape(3, -1)[None]
    hidden_pre = hidden_pre + fc1_bias.reshape(-1)[None]
    heads_here = mixed_pre.shape[2] // HEAD_DIM
    query_pre = mixed_pre[:, 0].reshape(tokens, heads_here, HEAD_DIM)
    key_pre = mixed_pre[:, 1].reshape(tokens, heads_here, HEAD_DIM)
    queries = rotary(query_pre, positions).astype(jnp.bfloat16)
    key_rows = rotary(key_pre, positions).astype(jnp.bfloat16)
    value_rows = mixed_pre[:, 2].reshape(tokens, heads_here, HEAD_DIM).astype(jnp.bfloat16)
    context_f, log_totals = attend_forward(queries, key_rows, value_rows, segment_ids)
    context = context_f.astype(jnp.bfloat16)
    hidden = jax.nn.gelu(hidden_pre, approximate=True).astype(jnp.bfloat16)
    context_rows, hidden_rows = (
        lax.all_gather(context, "row", axis=1, tiled=True),
        lax.all_gather(hidden, "row", axis=1, tiled=True),
    )
    partial_out = jnp.dot(context_rows, dense_weight, preferred_element_type=jnp.float32)
    partial_out = partial_out + jnp.dot(hidden_rows, fc2_weight, preferred_element_type=jnp.float32)
    summed_out = lax.psum_scatter(partial_out, "col", scatter_dimension=1, tiled=True)
    block_output = (
        block_input.astype(jnp.float32) + summed_out + dense_bias[None] + fc2_bias[None]
    ).astype(jnp.bfloat16)
    cot_float = cotangent.astype(jnp.float32)
    cot_rows = lax.all_gather(cotangent, "col", axis=1, tiled=True)
    dense_grad = jnp.einsum("ta,tb->ab", context_rows, cot_rows, preferred_element_type=jnp.float32)
    fc2_grad = jnp.einsum("ta,tb->ab", hidden_rows, cot_rows, preferred_element_type=jnp.float32)
    context_part = jnp.einsum(
        "tb,ab->ta", cot_rows, dense_weight, preferred_element_type=jnp.float32
    )
    hidden_part = jnp.einsum("tb,ab->ta", cot_rows, fc2_weight, preferred_element_type=jnp.float32)
    context_grad, hidden_grad = (
        lax.psum_scatter(context_part, "row", scatter_dimension=1, tiled=True),
        lax.psum_scatter(hidden_part, "row", scatter_dimension=1, tiled=True),
    )
    gelu_value, gelu_pull = jax.vjp(
        lambda values: jax.nn.gelu(values, approximate=True), hidden_pre
    )
    pre_grad = gelu_pull(hidden_grad)[0].astype(jnp.bfloat16)
    context_low = context_grad.astype(jnp.bfloat16).reshape(tokens, heads_here, HEAD_DIM)
    query_grad, key_grad, value_grad = attend_backward(
        queries, key_rows, value_rows, segment_ids, log_totals, context_low
    )
    query_value, query_pull = jax.vjp(lambda values: rotary(values, positions), query_pre)
    key_value, key_pull = jax.vjp(lambda values: rotary(values, positions), key_pre)
    mixed_grad = jnp.stack([query_pull(query_grad)[0], key_pull(key_grad)[0], value_grad], axis=1)
    mixed_grad = mixed_grad.reshape(tokens, 3, -1).astype(jnp.bfloat16)
    qkv_bias_grad = jnp.sum(mixed_grad.astype(jnp.float32), axis=0).reshape(qkv_bias.shape)
    fc1_bias_grad = jnp.sum(pre_grad.astype(jnp.float32), axis=0).reshape(fc1_bias.shape)
    mixed_rows, pre_rows = (
        lax.all_gather(mixed_grad, "row", axis=2, tiled=True),
        lax.all_gather(pre_grad, "row", axis=1, tiled=True),
    )
    qkv_grad = jnp.einsum(
        "td,tsk->dsk", normed_rows, mixed_rows, preferred_element_type=jnp.float32
    )
    up_grad = jnp.einsum("td,tk->dk", normed_rows, pre_rows, preferred_element_type=jnp.float32)
    normed_part = jnp.einsum(
        "tsk,dsk->td", mixed_rows, qkv_weight, preferred_element_type=jnp.float32
    )
    normed_part = normed_part + jnp.einsum(
        "tk,dk->td", pre_rows, fc1_weight, preferred_element_type=jnp.float32
    )
    normed_grad = lax.psum_scatter(normed_part, "col", scatter_dimension=1, tiled=True)
    slice_at = row_at * n_col + col_at
    scaled_here = lax.dynamic_slice_in_dim(centred_scaled, slice_at * part_width, part_width, 1)
    scaled_grad = normed_grad * ln_gain.astype(jnp.float32)[None]
    first_total, second_total = lax.psum(
        (jnp.sum(scaled_grad, axis=-1), jnp.sum(scaled_grad * scaled_here, axis=-1)), ("row", "col")
    )
    input_grad = cot_float + inv_std * (
        scaled_grad
        - first_total[:, None] / full_width
        - scaled_here * second_total[:, None] / full_width
    )
    gain_grad = jnp.sum(normed_grad * scaled_here, axis=0)
    shift_grad = jnp.sum(normed_grad, axis=0)
    bias_grad = jnp.sum(cot_float, axis=0)
    sums = lax.psum(
        (
            gain_grad,
            shift_grad,
            qkv_grad,
            qkv_bias_grad,
            dense_grad,
            bias_grad,
            up_grad,
            fc1_bias_grad,
            fc2_grad,
        ),
        "dp",
    )
    return (
        block_output,
        input_grad,
        sums[0],
        sums[1],
        sums[2],
        sums[3],
        sums[4],
        sums[5],
        sums[6],
        sums[7],
        sums[8],
        sums[5],
    )


def solution(mesh):
    return jax.shard_map(
        local,
        mesh=mesh,
        in_specs=(
            P("dp", ("row", "col")),
            P("dp"),
            P("dp"),
            P(("row", "col")),
            P(("row", "col")),
            P("row", None, "col"),
            P(None, "col", "row", None),
            P("col", "row"),
            P(("row", "col")),
            P("row", "col"),
            P("col", "row", None),
            P("col", "row"),
            P(("row", "col")),
            P("dp", ("row", "col")),
        ),
        out_specs=(
            P("dp", ("row", "col")),
            P("dp", ("row", "col")),
            P(("row", "col")),
            P(("row", "col")),
            P("row", None, "col"),
            P(None, "col", "row", None),
            P("col", "row"),
            P(("row", "col")),
            P("row", "col"),
            P("col", "row", None),
            P("col", "row"),
            P(("row", "col")),
        ),
        check_vma=False,
    )
```

profile of v0, /device:TPU:0, one launch (start us, length us, event | category | flops | bytes accessed | tf_op | source)
XLA Modules:
  0.0 1285.3 jit_solution(3277526663307692859)
XLA Ops:
  8.7 49.8 %all-gather.15.cloned.1.call-done = bf16[1024,1024]{1,0:T(8,128)(2,1)} async-done(((bf16[1024,256]{1,0:T(8,128)(2,1)}), bf16[1024,1024]{1,0:T(8,128)(2,1)}) %all-gather.15.cloned.1.call-update) | async-done | bytes 2097168 | tf_op jit(solution)/shard_map/all_gather | solution.py:182
  58.6 4.4 fusion.59
  63.1 17.9 %all-gather = bf16[8,1,256]{2,1,0:T(2,128)(2,1)S(1)} all-gather(bf16[1,1,256]{2,1,0:T(2,128)(2,1)S(1)} %reshape.268), channel_id=1, replica_groups=mesh['dp'=4,'row'=2,'col'=4] {'row','col'}, dimensions={0}, use_global_device_ids=true | all-gather | bytes 4608 | tf_op jit(solution)/shard_map/all_gather | solution.py:139
  81.1 16.9 %all-gather.1 = bf16[8,1,256]{2,1,0:T(2,128)(2,1)S(1)} all-gather(bf16[1,1,256]{2,1,0:T(2,128)(2,1)S(1)} %reshape.270), channel_id=1, replica_groups=mesh['dp'=4,'row'=2,'col'=4] {'row','col'}, dimensions={0}, use_global_device_ids=true | all-gather | bytes 4608 | tf_op jit(solution)/shard_map/all_gather | solution.py:140
  98.0 36.7 %all-gather.9.cloned.1.call-done = bf16[1024,2048]{1,0:T(8,128)(2,1)} async-done(((bf16[1024,256]{1,0:T(8,128)(2,1)}), bf16[1024,2048]{1,0:T(8,128)(2,1)}) %all-gather.9.cloned.1.call-update) | async-done | bytes 4194320 | tf_op jit(solution)/shard_map/all_gather | solution.py:138
  134.7 3.0 convert_reduce_fusion
  140.3 3.4 copy-done.6
  145.7 5.3 fusion.53
  151.0 10.8 fusion.60
  162.3 10.7 fusion.57
  178.3 68.6 %reduce-scatter.7.cloned.1.call-done = f32[1024,3,256]{2,0,1:T(8,128)} async-done(((f32[1024,3,512]{2,0,1:T(8,128)}), f32[1024,3,256]{2,0,1:T(8,128)}) %reduce-scatter.7.cloned.1.call-update) | async-done | bytes 3145744 | tf_op jit(solution)/shard_map/reduce_scatter | solution.py:157
  263.1 23.1 %while.28 = (s32[]{:T(128)}, bf16[2,512,4,64]{1,3,2,0:T(8,128)(2,1)}, f32[2,4,512]{2,1,0:T(4,128)}, s32[2]{0:T(128)S(1)}, s32[1024]{0:T(1024)S(1)}, /*index=5*/b...) while((s32[]{:T(128)}, ...), condition=%wide.region_6.7_spmd.clone, body=%wide.region_3.6_spmd.clone.sunk | while | flops 563608064 | bytes 35600724 | solution.py:67
  265.0 2.8 fusion.116
  270.2 3.0 fusion.118
  276.6 2.8 fusion.116
  281.8 3.0 fusion.118
  286.2 62.7 %reduce-scatter.15.cloned.1.call-done = f32[1024,1024]{1,0:T(8,128)} async-done(((f32[1024,2048]{1,0:T(8,128)}), f32[1024,1024]{1,0:T(8,128)}) %reduce-scatter.15.cloned.1.call-update) | async-done | bytes 4194320 | tf_op jit(solution)/shard_map/reduce_scatter | solution.py:191
  348.9 102.1 %reduce-scatter.9.cloned.1.call-done = f32[1024,1024]{1,0:T(8,128)} async-done(((f32[1024,2048]{1,0:T(8,128)}), f32[1024,1024]{1,0:T(8,128)}) %reduce-scatter.9.cloned.1.call-update) | async-done | bytes 4194320 | tf_op jit(solution)/shard_map/reduce_scatter | solution.py:158
  451.0 7.4 convert_reduce_fusion.1
  458.7 63.0 %while.29 = (s32[]{:T(128)}, f32[1024,4,64]{0,2,1:T(8,128)}, f32[1024,4,64]{0,2,1:T(8,128)}, f32[2,512,4,64]{1,0,3,2:T(2,128)}, s32[2]{0:T(128)S(1)}, /*index=5*...) while((s32[]{:T(128)}, f32[1024,4,64]{0,2,1:T(8,128)}, ...), condition=%wide.region_12.13_spmd.clone, body=%wide.region_10.12_spmd.clone.sunk | while | flops 1378351616 | bytes 91298248 | solution.py:107
  465.1 3.5 fusion.131
  468.6 3.2 multiply_reduce_fusion.5
  479.2 10.4 dynamic_update_slice.21
  496.0 4.6 fusion.131
  500.5 3.2 multiply_reduce_fusion.5
  511.2 10.4 dynamic_update_slice.21
  521.8 3.1 reshape.265
  541.0 2.8 convert_reduce_fusion.2
  547.2 10.3 fusion.61
  557.6 31.4 %all-gather.17.cloned.1.call-done = bf16[1024,3,512]{2,0,1:T(8,128)(2,1)} async-done(((bf16[1024,3,256]{2,0,1:T(8,128)(2,1)}), bf16[1024,3,512]{2,0,1:T(8,128)(2,1)}) %all-gather.17.cloned.1.call-update) | async-done | bytes 3145744 | tf_op jit(solution)/shard_map/all_gather | solution.py:208
  589.0 7.6 bitcast_add_fusion
  596.6 51.2 %all-gather.13.cloned.1.call-done = bf16[1024,2048]{1,0:T(8,128)(2,1)} async-done(((bf16[1024,1024]{1,0:T(8,128)(2,1)}), bf16[1024,2048]{1,0:T(8,128)(2,1)}) %all-gather.13.cloned.1.call-update) | async-done | bytes 4194320 | tf_op jit(solution)/shard_map/all_gather | solution.py:173
  647.9 10.0 fusion.58
  657.8 13.3 %all-gather.11.cloned.1.call-done = bf16[1024,512]{0,1:T(8,128)(2,1)} async-done(((bf16[1024,256]{0,1:T(8,128)(2,1)}), bf16[1024,512]{0,1:T(8,128)(2,1)}) %all-gather.11.cloned.1.call-update) | async-done | bytes 1048592 | tf_op jit(solution)/shard_map/all_gather | solution.py:172
  671.2 6.1 convolution_add_fusion
  677.6 4.9 fusion.62
  682.5 5.4 fusion.51
  688.0 6.8 fusion.64
  694.8 6.8 fusion.63
  702.2 48.0 %reduce-scatter.17.cloned.1.call-done = f32[1024,256]{1,0:T(8,128)} async-done(((f32[1024,1024]{1,0:T(8,128)}), f32[1024,256]{1,0:T(8,128)}) %reduce-scatter.17.cloned.1.call-update) | async-done | bytes 1048592 | tf_op jit(solution)/shard_map/reduce_scatter | solution.py:221
  752.2 21.9 %all-reduce.6 = (f32[1024]{0:T(1024)S(1)}, f32[1024]{0:T(1024)S(1)}) all-reduce(f32[1024]{0:T(1024)S(1)} %get-tuple-element.205, f32[1024]{0:T(1024)S(1)} %get-tuple-element.206), channel_id=1, replica_groups=mesh['dp'=4,'row'=2,'col'=4] {'row','col'}, use_global_device_ids=true, to_apply=%region_18.19 | all-reduce | flops 2048 | bytes 16384 | tf_op jit(solution)/shard_map/psum | solution.py:225
  774.2 3.2 convert_reduce_fusion.3
  777.4 11.5 all-reduce.7
  788.9 41.7 %reduce-scatter.11.cloned.1.call-done = f32[1024,256]{1,0:T(8,128)} async-done(((f32[1024,1024]{1,0:T(8,128)}), f32[1024,256]{1,0:T(8,128)}) %reduce-scatter.11.cloned.1.call-update) | async-done | bytes 1048592 | tf_op jit(solution)/shard_map/reduce_scatter | solution.py:177
  832.9 427.0 %all-reduce.11.cloned.1.call-done = (f32[1024,3,512]{2,0,1:T(8,128)}, f32[512,1024]{1,0:T(8,128)}, f32[1024,2048]{1,0:T(8,128)}, f32[2048,1024]{1,0:T(8,128)}) async-done(((f32[1024,3,512]{2,0,1:T(8,128)}, f32[512,1024]{1,0:T(8,128)}, f32[1024,2048]{1,0:T(8,128)}, f32[2048,1024]{1,0:T(8,128)}), (f32[1024,3,512]{2,0,1:T(8,128)}, f32[512,1024]{1,0:T(8,128)}, f32[1024,2048]{1,0:T(8,128)}, ...) | async-done | bytes 25165840 | tf_op jit(solution)/shard_map/psum | solution.py:236
  1260.5 6.9 copy.114
  1269.1 4.3 copy.116
  1274.9 3.4 copy.117
  (218 shorter events, 89.2 us)
Async XLA Ops:
  7.2 138.5 %copy-start = (bf16[1024,3,512]{2,0,1:T(8,128)(2,1)S(1)}, bf16[1024,3,512]{2,0,1:T(8,128)(2,1)}, u32[]{:S(2)}) copy-start(bf16[1024,3,512]{2,0,1:T(8,128)(2,1)} %param.23) | copy-start | bytes 9437188
  7.2 51.4 %all-gather.15.cloned.1.call-start = ((), (), s32[]{:S(2)}) async-start(), calls=%async_computation.12 | async-start | bytes 2621440 | tf_op jit(solution)/shard_map/all_gather | solution.py:182
  7.9 126.8 %all-gather.9.cloned.1.call-start = ((), (), s32[]{:S(2)}) async-start(), calls=%async_computation.6 | async-start | bytes 4718592 | tf_op jit(solution)/shard_map/all_gather | solution.py:138
  8.7 54.4 %copy-start.37 = (bf16[256]{0:T(256)(128)(2,1)S(1)}, bf16[256]{0:T(256)(128)(2,1)}, u32[]{:S(2)}) copy-start(bf16[256]{0:T(256)(128)(2,1)} %param.22) | copy-start | bytes 1540
  8.7 54.4 %copy-start.38 = (bf16[256]{0:T(256)(128)(2,1)S(1)}, bf16[256]{0:T(256)(128)(2,1)}, u32[]{:S(2)}) copy-start(bf16[256]{0:T(256)(128)(2,1)} %param.21) | copy-start | bytes 1540
  8.7 165.4 %reduce-scatter.13.cloned.1.call-start = ((), (), s32[]{:S(2)}) async-start(), calls=%async_computation.13 | async-start | bytes 3145728 | tf_op jit(solution)/shard_map/reduce_scatter | solution.py:190
  63.0 183.9 %reduce-scatter.7.cloned.1.call-start = ((), (), s32[]{:S(2)}) async-start(), calls=%async_computation.7 | async-start | bytes 9437184 | tf_op jit(solution)/shard_map/reduce_scatter | solution.py:157
  134.7 3.4 copy-start.5
  140.3 3.4 copy-start.6
  150.9 198.0 %reduce-scatter.15.cloned.1.call-start = ((), (), s32[]{:S(2)}) async-start(), calls=%async_computation.15 | async-start | bytes 12582912 | tf_op jit(solution)/shard_map/reduce_scatter | solution.py:191
  161.8 289.2 %reduce-scatter.9.cloned.1.call-start = ((), (), s32[]{:S(2)}) async-start(), calls=%async_computation.9 | async-start | bytes 12582912 | tf_op jit(solution)/shard_map/reduce_scatter | solution.py:158
  173.0 374.2 %all-gather.19.cloned.1.call-start = ((), (), s32[]{:S(2)}) async-start(), calls=%async_computation.16 | async-start | bytes 6291456 | tf_op jit(solution)/shard_map/all_gather | solution.py:209
  174.0 86.7 %copy-start.15 = (f32[1024,16]{0,1:T(8,128)}, f32[1024,16]{0,1:T(8,128)S(1)}, u32[]{:S(2)}) copy-start(f32[1024,16]{0,1:T(8,128)S(1)} %get-tuple-element.282) | copy-start | bytes 196612
  174.0 86.7 %copy-start.17 = (f32[1024,16]{0,1:T(8,128)}, f32[1024,16]{0,1:T(8,128)S(1)}, u32[]{:S(2)}) copy-start(f32[1024,16]{0,1:T(8,128)S(1)} %get-tuple-element.283) | copy-start | bytes 196612
  253.9 9.2 copy-start.14
  263.1 187.9 %copy-start.27 = (f32[1,1,1024]{2,1,0:T(1,128)S(1)}, f32[1,1,1024]{2,1,0:T(1,128)}, u32[]{:S(2)}) copy-start(f32[1,1,1024]{2,1,0:T(1,128)} %param.28) | copy-start | bytes 12292
  270.2 3.0 copy-start.21
  279.4 2.4 copy-start.19
  281.8 3.0 copy-start.21
  451.0 7.7 copy-start.23
  458.5 130.5 %all-gather.17.cloned.1.call-start = ((), (), s32[]{:S(2)}) async-start(), calls=%async_computation.14 | async-start | bytes 4718592 | tf_op jit(solution)/shard_map/all_gather | solution.py:208
  462.6 2.5 copy-start.10
  465.1 3.5 copy-start.8
  471.8 2.7 copy-start.1
  493.5 2.5 copy-start.10
  496.0 4.6 copy-start.8
  503.7 2.7 copy-start.1
  521.8 6.1 copy-start.16
  521.8 6.1 copy-start.18
  543.9 104.0 %all-gather.13.cloned.1.call-start = ((), (), s32[]{:S(2)}) async-start(), calls=%async_computation.10 | async-start | bytes 6291456 | tf_op jit(solution)/shard_map/all_gather | solution.py:173
  544.6 126.5 %all-gather.11.cloned.1.call-start = ((), (), s32[]{:S(2)}) async-start(), calls=%async_computation.8 | async-start | bytes 1572864 | tf_op jit(solution)/shard_map/all_gather | solution.py:172
  547.2 203.1 %reduce-scatter.17.cloned.1.call-start = ((), (), s32[]{:S(2)}) async-start(), calls=%async_computation.17 | async-start | bytes 5242880 | tf_op jit(solution)/shard_map/reduce_scatter | solution.py:221
  596.6 234.0 %reduce-scatter.11.cloned.1.call-start = ((), (), s32[]{:S(2)}) async-start(), calls=%async_computation.11 | async-start | bytes 5242880 | tf_op jit(solution)/shard_map/reduce_scatter | solution.py:177
  677.3 582.7 %all-reduce.11.cloned.1.call-start = ((), (), s32[]{:S(2)}) async-start(), calls=%async_computation.18 | async-start | bytes 50331648 | tf_op jit(solution)/shard_map/psum | solution.py:236
  677.6 4.9 copy-start.12
  677.6 4.9 copy-start.35
  682.5 5.5 copy-start.34
  682.5 5.5 copy-start.36
  688.0 6.8 copy-start.33
  701.6 72.6 %copy-start.25 = (f32[1024]{0:T(1024)S(1)}, f32[1024]{0:T(1024)}, u32[]{:S(2)}) copy-start(f32[1024]{0:T(1024)} %copy-done.24) | copy-start | bytes 12292
  701.6 75.8 %copy-start.26 = (f32[1024]{0:T(1024)S(1)}, f32[1024]{0:T(1024)}, u32[]{:S(2)}) copy-start(f32[1024]{0:T(1024)} %get-tuple-element.257) | copy-start | bytes 12292
  701.6 129.0 %copy-start.30 = (f32[256]{0:T(256)S(1)}, f32[256]{0:T(256)}, u32[]{:S(2)}) copy-start(f32[256]{0:T(256)} %param.30) | copy-start | bytes 3076
  701.6 129.0 %copy-start.31 = (f32[256]{0:T(256)S(1)}, f32[256]{0:T(256)}, u32[]{:S(2)}) copy-start(f32[256]{0:T(256)} %param.26) | copy-start | bytes 3076
  788.9 478.5 %copy-start.32 = (f32[256]{0:T(256)}, f32[256]{0:T(256)S(1)}, u32[]{:S(2)}) copy-start(f32[256]{0:T(256)S(1)} %get-tuple-element.525) | copy-start | bytes 3076
  1260.5 6.9 copy-start.13
  1260.5 8.6 copy-start.9
  1267.4 5.9 slice-start
  1269.1 5.8 slice-start.1
  (18 other events, 22.0 us)
Sparse Core Ops, SparseCore 0:
  9.6 48.9 all-gather.14
  60.6 74.0 all-gather.8
  136.9 29.9 reduce-scatter.12
  169.8 77.0 reduce-scatter.6
  249.6 99.2 reduce-scatter.14
  351.7 99.2 reduce-scatter.8
  458.6 56.7 all-gather.18
  544.0 44.8 all-gather.16
  591.1 56.7 all-gather.12
  649.8 21.2 all-gather.10
  673.5 76.7 reduce-scatter.16
  752.5 78.0 reduce-scatter.10
  834.5 425.4 all-reduce.10
where the time goes:
time: 1300 us; the launch traced here: 1290 us
  waiting for transfers between devices  935 us (72%)
  matrix products  125 us (10%)
  local copies, waits for them, and re-layouts  84.2 us (6%)
  blocking collectives  68.2 us (5%)
  other arithmetic  49.8 us (4%)
  between operations  14.8 us (1%)
    psum x1, waiting for transfers between devices, local(): lax.psum((gain_grad, shift_grad, qkv_grad, qkv_bias_grad, dense_grad, bia...  427 us
    reduce_scatter x1, waiting for transfers between devices, local(): lax.psum_scatter(part_up, 'row', scatter_dimension=1, tiled=True)  102 us
    reduce_scatter x1, waiting for transfers between devices, local(): lax.psum_scatter(part_qkv, 'row', scatter_dimension=2, tiled=True)  68.6 us
    reduce_scatter x1, waiting for transfers between devices, local(): lax.psum_scatter(hidden_part, 'row', scatter_dimension=1, tiled=True)  62.7 us
    all_gather x1, waiting for transfers between devices, local(): lax.all_gather(hidden, 'row', axis=1, tiled=True)  51.2 us
    all_gather x1, waiting for transfers between devices, local(): cot_rows = lax.all_gather(cotangent, 'col', axis=1, tiled=True)  49.8 us
    reduce_scatter x1, waiting for transfers between devices, local(): lax.psum_scatter(normed_part, 'col', scatter_dimension=1, tiled=True)  48 us
    reduce_scatter x1, waiting for transfers between devices, local(): lax.psum_scatter(partial_out, 'col', scatter_dimension=1, tiled=True)  41.7 us
  transfers between devices with their start and end apart: 13, of which 11 were waited for; matrix products, arithmetic and copies ran while one was open for 17% of the time, Pallas kernels for 0%

commit v1 on v0

v1 whole, which is shorter than its diff:
```python
import functools
import math

import jax
import jax.numpy as jnp
from jax import lax
from jax.experimental import pallas as pl
from jax.experimental.pallas import tpu as pltpu
from jax.sharding import PartitionSpec as P

HEAD_DIM = 64
ROT_DIM = 32
NORM_EPSILON = 1e-05
MASKED_SCORE = -1e30
QUERY_ROWS = 256
MESH = pl.DeviceIdType.MESH
BF = jnp.bfloat16
F32 = jnp.float32


def gather_kernel(
    n_col,
    x_ref,
    cot_ref,
    gb_ref,
    wq_ref,
    w1_ref,
    w2_ref,
    wd_ref,
    xf_ref,
    cf_ref,
    gf_ref,
    qf_ref,
    f1_ref,
    f2_ref,
    df_ref,
    x_send,
    x_recv,
    g_send,
    g_recv,
    c_send,
    c_recv,
    cx_send,
    cx_recv,
    w_send,
    w_recv,
    s_send,
    s_recv,
    own_sem,
    *staged,
):
    d = lax.axis_index("dp")
    r = lax.axis_index("row")
    c = lax.axis_index("col")
    core = lax.rem(d, 2)
    sibling = d + 1 - 2 * core
    other = 1 - r
    has_right = c < n_col - 1
    has_left = c > 0
    right = jnp.minimum(c + 1, n_col - 1)
    left = jnp.maximum(c - 1, 0)
    width = x_ref.shape[1]

    def to(dd, rr, cc):
        return dict(device_id=(dd, rr, cc), device_id_type=MESH)

    barrier = pltpu.get_barrier_semaphore()
    pl.semaphore_signal(barrier, inc=1, **to(d, other, c))
    pl.semaphore_signal(barrier, inc=1, **to(sibling, r, c))

    @pl.when(has_right)
    def _():
        pl.semaphore_signal(barrier, inc=1, **to(d, r, right))

    @pl.when(has_left)
    def _():
        pl.semaphore_signal(barrier, inc=1, **to(d, r, left))

    pl.semaphore_wait(barrier, 2 + has_right.astype(jnp.int32) + has_left.astype(jnp.int32))

    def block(ref, rr, j):
        start = pl.multiple_of((rr * n_col + j) * width, width)
        return ref.at[:, pl.ds(start, width)]

    def hop(full, own, rr, j, send, recv, lane, step):
        dst = block(full, rr, j)
        src = dst if own is None else own
        cc = right if step == 0 else left
        return pltpu.make_async_remote_copy(
            src_ref=src,
            dst_ref=dst,
            send_sem=send.at[lane, step, j],
            recv_sem=recv.at[lane, j],
            **to(d, r, cc),
        )

    def across(full, own, j, send, recv):
        dst = block(full, r, j)
        return pltpu.make_async_remote_copy(
            src_ref=dst if own is None else own,
            dst_ref=dst,
            send_sem=send,
            recv_sem=recv,
            **to(d, other, c),
        )

    def arrived(full, rr, j, recv):
        dst = block(full, rr, j)
        return pltpu.make_async_remote_copy(
            src_ref=dst, dst_ref=dst, send_sem=recv, recv_sem=recv, **to(d, other, c)
        )

    def start_both(full, own, rr, send, recv, lane):
        @pl.when(has_right)
        def _():
            hop(full, own, rr, c, send, recv, lane, 0).start()

        @pl.when(has_left)
        def _():
            hop(full, own, rr, c, send, recv, lane, 1).start()

    def advance(full, rr, send, recv, lane, s, then=None):
        @pl.when(c >= s)
        def _():
            j = c - s
            arrived(full, rr, j, recv.at[lane, j]).wait_recv()

            @pl.when(has_right)
            def _():
                hop(full, None, rr, j, send, recv, lane, 0).start()

            if then is not None:
                then(j)

        @pl.when(c + s < n_col)
        def _():
            j = c + s
            arrived(full, rr, j, recv.at[lane, j]).wait_recv()

            @pl.when(has_left)
            def _():
                hop(full, None, rr, j, send, recv, lane, 1).start()

            if then is not None:
                then(j)

    def drain(full, rr, send, recv, lane):
        for s in range(n_col):

            @pl.when((c >= s) & has_right)
            def _():
                hop(full, None, rr, jnp.maximum(c - s, 0), send, recv, lane, 0).wait_send()

            @pl.when((c + s < n_col) & has_left)
            def _():
                j = jnp.minimum(c + s, n_col - 1)
                hop(full, None, rr, j, send, recv, lane, 1).wait_send()

    def pieces(k, rr):
        out = []
        depth = wq_ref.shape[1] // 2
        part = wq_ref.shape[2] // 2
        for s in range(3):
            out.append(
                (
                    wq_ref.at[s, pl.ds(k * depth, depth), pl.ds((1 - rr) * part, part)],
                    qf_ref.at[pl.ds(rr * 2 * depth + k * depth, depth), pl.ds(s * part, part)],
                )
            )
        depth = w1_ref.shape[0] // 2
        part = w1_ref.shape[1] // 2
        out.append(
            (
                w1_ref.at[pl.ds(k * depth, depth), pl.ds((1 - rr) * part, part)],
                f1_ref.at[pl.ds(rr * 2 * depth + k * depth, depth), :],
            )
        )
        half = w2_ref.shape[0] // 2
        depth = half // 2
        part = w2_ref.shape[1]
        out.append(
            (
                w2_ref.at[pl.ds((1 - rr) * half + k * depth, depth), :],
                f2_ref.at[pl.ds(k * depth, depth), pl.ds(rr * part, part)],
            )
        )
        half = wd_ref.shape[0] // 2
        depth = half // 2
        part = wd_ref.shape[1]
        out.append(
            (
                wd_ref.at[pl.ds((1 - rr) * half + k * depth, depth), :],
                df_ref.at[pl.ds(k * depth, depth), pl.ds(rr * part, part)],
            )
        )
        return out

    n_piece = 6

    def weight_across(i):
        src, dst = pieces(core, r)[i]
        return pltpu.make_async_remote_copy(
            src_ref=src, dst_ref=dst, send_sem=w_send.at[i], recv_sem=w_recv.at[i], **to(d, other, c)
        )

    def weight_landed(i):
        dst = pieces(core, other)[i][1]
        return pltpu.make_async_remote_copy(
            src_ref=dst, dst_ref=dst, send_sem=w_send.at[i], recv_sem=w_recv.at[i], **to(d, other, c)
        )

    def weight_share(i):
        dst = pieces(core, other)[i][1]
        return pltpu.make_async_remote_copy(
            src_ref=dst, dst_ref=dst, send_sem=s_send.at[i], recv_sem=s_recv.at[i], **to(sibling, r, c)
        )

    def weight_shared(i):
        dst = pieces(1 - core, other)[i][1]
        return pltpu.make_async_remote_copy(
            src_ref=dst, dst_ref=dst, send_sem=s_send.at[i], recv_sem=s_recv.at[i], **to(sibling, r, c)
        )

    part = wq_ref.shape[2] // 2
    depth = wq_ref.shape[1]
    own = [(x_ref, block(xf_ref, r, c)), (cot_ref, block(cf_ref, r, c)), (gb_ref, block(gf_ref, r, c))]
    for s in range(3):
        own.append(
            (
                wq_ref.at[s, :, pl.ds(r * part, part)],
                qf_ref.at[pl.ds(r * depth, depth), pl.ds(s * part, part)],
            )
        )
    depth = w1_ref.shape[0]
    part = w1_ref.shape[1] // 2
    own.append((w1_ref.at[:, pl.ds(r * part, part)], f1_ref.at[pl.ds(r * depth, depth), :]))
    for src, dst in ((w2_ref, f2_ref), (wd_ref, df_ref)):
        depth = src.shape[0] // 2
        part = src.shape[1]
        own.append((src.at[pl.ds(r * depth, depth), :], dst.at[:, pl.ds(r * part, part)]))
    own_in = [pltpu.make_async_copy(a, v, own_sem.at[0, i]) for i, ((a, b), v) in enumerate(zip(own, staged))]
    own_out = [pltpu.make_async_copy(v, b, own_sem.at[1, i]) for i, ((a, b), v) in enumerate(zip(own, staged))]

    gb_across = across(gf_ref, gb_ref, c, g_send.at[1, 2, c], g_recv.at[1, c])
    x_across = across(xf_ref, x_ref, c, x_send.at[1, 2, c], x_recv.at[1, c])
    gb_across.start()
    x_across.start()
    start_both(gf_ref, gb_ref, r, g_send, g_recv, 0)
    start_both(xf_ref, x_ref, r, x_send, x_recv, 0)
    for copy in own_in:
        copy.start()

    for arrive, leave in zip(own_in, own_out):
        arrive.wait()
        leave.start()

    arrived(gf_ref, other, c, g_recv.at[1, c]).wait_recv()
    start_both(gf_ref, None, other, g_send, g_recv, 1)
    arrived(xf_ref, other, c, x_recv.at[1, c]).wait_recv()
    start_both(xf_ref, None, other, x_send, x_recv, 1)
    cot_across = lambda j: across(cf_ref, None, j, cx_send.at[j], cx_recv.at[j])
    across(cf_ref, cot_ref, c, cx_send.at[c], cx_recv.at[c]).start()
    for i in range(n_piece):
        weight_across(i).start()
    start_both(cf_ref, cot_ref, r, c_send, c_recv, 0)
    for s in range(1, n_col):
        for lane in range(2):
            rr = r if lane == 0 else other
            advance(gf_ref, rr, g_send, g_recv, lane, s)
            advance(xf_ref, rr, x_send, x_recv, lane, s)
        advance(cf_ref, r, c_send, c_recv, 0, s, then=lambda j: cot_across(j).start())
    for i in range(n_piece):
        weight_landed(i).wait_recv()
        weight_share(i).start()
    for s in range(n_col):
        arrived(cf_ref, other, s, cx_recv.at[s]).wait_recv()
        cot_across(s).wait_send()
    for i in range(n_piece):
        weight_shared(i).wait_recv()
        weight_across(i).wait_send()
        weight_share(i).wait_send()
    for lane in range(2):
        rr = r if lane == 0 else other
        drain(gf_ref, rr, g_send, g_recv, lane)
        drain(xf_ref, rr, x_send, x_recv, lane)
    drain(cf_ref, r, c_send, c_recv, 0)
    gb_across.wait_send()
    x_across.wait_send()
    for copy in own_out:
        copy.wait()


def gather_all(n_row, n_col, x, cot, gb, wq, w1, w2, wd):
    tokens, width = x.shape
    full = width * n_row * n_col
    hbm = pl.BlockSpec(memory_space=pl.ANY)
    dma = pltpu.SemaphoreType.DMA
    shapes = (
        ((tokens, full), BF),
        ((tokens, full), BF),
        ((gb.shape[0], full), F32),
        ((wq.shape[1] * n_row, 3 * wq.shape[2] // n_row), BF),
        ((w1.shape[0] * n_row, w1.shape[1] // n_row), BF),
        ((w2.shape[0] // n_row, w2.shape[1] * n_row), BF),
        ((wd.shape[0] // n_row, wd.shape[1] * n_row), BF),
    )
    return pl.pallas_call(
        functools.partial(gather_kernel, n_col),
        out_shape=tuple(jax.ShapeDtypeStruct(s, t) for s, t in shapes),
        in_specs=[hbm] * 7,
        out_specs=(hbm,) * 7,
        scratch_shapes=[
            dma((2, 3, n_col)),
            dma((2, n_col)),
            dma((2, 3, n_col)),
            dma((2, n_col)),
            dma((1, 2, n_col)),
            dma((1, n_col)),
            dma((n_col,)),
            dma((n_col,)),
            dma((6,)),
            dma((6,)),
            dma((6,)),
            dma((6,)),
            dma((2, 9)),
            pltpu.VMEM(x.shape, BF),
            pltpu.VMEM(cot.shape, BF),
            pltpu.VMEM(gb.shape, F32),
        ]
        + [pltpu.VMEM((wq.shape[1], wq.shape[2] // n_row), BF)] * 3
        + [
            pltpu.VMEM((w1.shape[0], w1.shape[1] // n_row), BF),
            pltpu.VMEM((w2.shape[0] // n_row, w2.shape[1]), BF),
            pltpu.VMEM((wd.shape[0] // n_row, wd.shape[1]), BF),
        ],
        compiler_params=pltpu.CompilerParams(
            collective_id=0, has_side_effects=True, vmem_limit_bytes=24 * 2**20
        ),
        cost_estimate=pl.CostEstimate(flops=0, bytes_accessed=300 * 2**20, transcendentals=0),
    )(x, cot, gb, wq, w1, w2, wd)


def attention_kernel(
    mixed_ref,
    grad_ref,
    cos_ref,
    sin_ref,
    seg_col_ref,
    seg_row_ref,
    ctx_ref,
    out_ref,
    q_s,
    k_s,
    v_s,
    dk_s,
    dv_s,
    bias_s,
    *,
    query_rows,
):
    tokens, width = grad_ref.shape
    pairs = width // 128
    scale = HEAD_DIM**-0.5
    lane = lax.broadcasted_iota(jnp.int32, (1, 128), 1)
    first = lane % HEAD_DIM < ROT_DIM // 2
    low_head = lane < HEAD_DIM
    contract_last = (((1,), (1,)), ((), ()))
    contract_first = (((0,), (0,)), ((), ()))

    def turn(v, cos, sin, sign):
        up = pltpu.roll(v, 128 - ROT_DIM // 2, 1)
        down = pltpu.roll(v, ROT_DIM // 2, 1)
        swapped = jnp.where(first, -up, down) * sin
        return v * cos + swapped if sign > 0 else v * cos - swapped

    for t in range(pairs):
        cos, sin = cos_ref[...], sin_ref[...]
        at = slice(t * 128, (t + 1) * 128)
        q_s[t] = turn(mixed_ref[0, :, at], cos, sin, 1).astype(BF)
        k_s[t] = turn(mixed_ref[1, :, at], cos, sin, 1).astype(BF)
        v_s[t] = mixed_ref[2, :, at].astype(BF)
    dk_s[...] = jnp.zeros_like(dk_s)
    dv_s[...] = jnp.zeros_like(dv_s)
    for i in range(tokens // query_rows):
        keys = (i + 1) * query_rows
        rows = slice(i * query_rows, keys)
        row_at = lax.broadcasted_iota(jnp.int32, (query_rows, keys), 0) + i * query_rows
        key_at = lax.broadcasted_iota(jnp.int32, (query_rows, keys), 1)
        allowed = (seg_col_ref[rows, :] == seg_row_ref[:, :keys]) & (row_at >= key_at)
        bias_s[:, :keys] = jnp.where(allowed, 0.0, MASKED_SCORE)

        def pair(t, carry):
            at = pl.ds(pl.multiple_of(t * 128, 128), 128)
            q, k, v = q_s[t, rows, :], k_s[t, :keys, :], v_s[t, :keys, :]
            grad = grad_ref[rows, at]
            outs, query_grads = [], []
            for h in range(2):
                mine = low_head if h == 0 else ~low_head
                qh = jnp.where(mine, q, jnp.zeros_like(q))
                gh = jnp.where(mine, grad, jnp.zeros_like(grad))
                s = lax.dot_general(qh, k, contract_last, preferred_element_type=F32)
                s = s * scale + bias_s[:, :keys]
                e = jnp.exp(s - jnp.max(s, axis=1, keepdims=True))
                p = e * (1.0 / jnp.sum(e, axis=1, keepdims=True))
                low = p.astype(BF)
                outs.append(jnp.dot(low, v, preferred_element_type=F32))
                dp = lax.dot_general(gh, v, contract_last, preferred_element_type=F32)
                centre = jnp.sum(p * dp, axis=1, keepdims=True)
                ds = (p * (dp - centre) * scale).astype(BF)
                query_grads.append(jnp.dot(ds, k, preferred_element_type=F32))
                dk_s[t, :keys, :] += lax.dot_general(
                    ds, qh, contract_first, preferred_element_type=F32
                )
                dv_s[t, :keys, :] += lax.dot_general(
                    low, gh, contract_first, preferred_element_type=F32
                )
            ctx_ref[rows, at] = jnp.where(low_head, outs[0], outs[1]).astype(BF)
            dq = jnp.where(low_head, query_grads[0], query_grads[1])
            out_ref[rows, at] = turn(dq, cos_ref[rows, :], sin_ref[rows, :], -1).astype(BF)
            return carry

        lax.fori_loop(0, pairs, pair, 0)
    for t in range(pairs):
        at = width + t * 128
        out_ref[:, at : at + 128] = turn(dk_s[t], cos_ref[...], sin_ref[...], -1).astype(BF)
        at = 2 * width + t * 128
        out_ref[:, at : at + 128] = dv_s[t].astype(BF)


def attention(mixed, context_grad, cos, sin, segments):
    tokens, width = context_grad.shape
    pairs = width // 128
    vmem = pl.BlockSpec(memory_space=pltpu.VMEM)
    return pl.pallas_call(
        functools.partial(attention_kernel, query_rows=min(QUERY_ROWS, tokens)),
        out_shape=(
            jax.ShapeDtypeStruct((tokens, width), BF),
            jax.ShapeDtypeStruct((tokens, 3 * width), BF),
        ),
        in_specs=[vmem] * 6,
        out_specs=(vmem, vmem),
        scratch_shapes=[pltpu.VMEM((pairs, tokens, 128), BF)] * 3
        + [pltpu.VMEM((pairs, tokens, 128), F32)] * 2
        + [pltpu.VMEM((min(QUERY_ROWS, tokens), tokens), F32)],
        compiler_params=pltpu.CompilerParams(
            vmem_limit_bytes=56 * 2**20, fuse_transposed_lhs_in_matmul=True
        ),
        cost_estimate=pl.CostEstimate(
            flops=2 * 10**10, bytes_accessed=64 * 2**20, transcendentals=3 * 2**20
        ),
    )(mixed, context_grad, cos, sin, segments.reshape(tokens, 1), segments.reshape(1, tokens))


def rotation_tables(positions):
    half = ROT_DIM // 2
    steps = jnp.arange(half).astype(F32)
    frequency = jnp.exp(steps * (-2.0 * math.log(10000.0) / ROT_DIM))
    angles = positions.astype(F32)[:, None] * frequency[None, :]
    cos, sin = jnp.cos(angles), jnp.sin(angles)
    rest = (positions.shape[0], HEAD_DIM - ROT_DIM)
    return (
        jnp.concatenate([cos, cos, jnp.ones(rest, F32)] * (128 // HEAD_DIM), axis=1),
        jnp.concatenate([sin, sin, jnp.zeros(rest, F32)] * (128 // HEAD_DIM), axis=1),
    )


def swap_row(value):
    return lax.ppermute(value, "row", [(0, 1), (1, 0)])


def swap_dp(value, bit):
    n = lax.axis_size("dp")
    return lax.ppermute(value, "dp", [(i, i ^ (1 << bit)) for i in range(n)])


def dp_bits():
    return lax.axis_size("dp").bit_length() - 1


def take(value, at):
    return lax.dynamic_index_in_dim(value, at, 1, keepdims=False)


def reduce_dp(grad):
    n = lax.axis_size("dp")
    d = lax.axis_index("dp")
    width = grad.shape[1]
    rows = grad.shape[0] // n
    cur = grad
    for bit in range(dp_bits()):
        mine = (d >> bit) & 1
        left = n >> (bit + 1)
        parts = cur.reshape(left, 2, rows, width)
        got = swap_dp(take(parts, 1 - mine).astype(BF), bit)
        cur = (take(parts, mine) + got.astype(F32)).reshape(-1, width)
    return cur


def spread_dp(pieces):
    everyone = [pieces]
    for bit in reversed(range(dp_bits())):
        got = [[swap_dp(p, bit) for p in ps] for ps in everyone]
        everyone = everyone + got
    return everyone


def spread_order():
    order = [0]
    for bit in reversed(range(dp_bits())):
        order = order + [o ^ (1 << bit) for o in order]
    return order


def sum_all_dp(value):
    for bit in range(dp_bits()):
        value = value + swap_dp(value, bit)
    return value


def scatter_group(mine, theirs):
    n_col = lax.axis_size("col")
    c = lax.axis_index("col")
    total = mine + swap_row(theirs.astype(BF)).astype(F32)
    width = total.shape[1] // n_col

    def chunk(shift):
        at = lax.rem(c + shift, n_col) * width
        return lax.dynamic_slice_in_dim(total, at, width, 1)

    got = [
        lax.ppermute(
            chunk(s).astype(BF), "col", [(i, (i + s) % n_col) for i in range(n_col)]
        ).astype(F32)
        for s in range(1, n_col)
    ]
    out = chunk(0)
    for g in got:
        out = out + g
    return out


def local(
    block_input,
    segment_ids,
    positions,
    ln_gain,
    ln_bias,
    qkv_weight,
    qkv_bias,
    dense_weight,
    dense_bias,
    fc1_weight,
    fc1_bias,
    fc2_weight,
    fc2_bias,
    cotangent,
):
    n_row = lax.axis_size("row")
    n_col = lax.axis_size("col")
    n_dp = lax.axis_size("dp")
    r = lax.axis_index("row")
    c = lax.axis_index("col")
    d = lax.axis_index("dp")
    tokens, part_width = block_input.shape
    full_width = part_width * n_row * n_col
    half_width = full_width // n_row
    mine_at = r * half_width
    theirs_at = (1 - r) * half_width

    gb = jnp.concatenate(
        [
            jnp.broadcast_to(ln_gain.astype(F32)[None], (8, part_width)),
            jnp.broadcast_to(ln_bias.astype(F32)[None], (8, part_width)),
        ],
        axis=0,
    )
    whole, cot, gb_full, wq, w1, w2, wd = gather_all(
        n_row,
        n_col,
        block_input,
        cotangent,
        gb,
        jnp.transpose(qkv_weight, (1, 0, 2)),
        fc1_weight,
        fc2_weight,
        dense_weight,
    )
    gain = gb_full[0:1]
    shift = gb_full[8:9]
    whole_f = whole.astype(F32)
    row_mean = jnp.mean(whole_f, axis=-1, keepdims=True)
    variance = jnp.mean(jnp.square(whole_f - row_mean), axis=-1, keepdims=True)
    inv_std = lax.rsqrt(variance + NORM_EPSILON)
    normed = ((whole_f - row_mean) * inv_std * gain + shift).astype(BF)

    def dot(a, b, dims):
        return lax.dot_general(a, b, (dims, ((), ())), preferred_element_type=F32)

    nn = ((1,), (0,))
    nt = ((1,), (1,))
    tn = ((0,), (0,))

    def cols(a, at, size):
        return lax.dynamic_slice_in_dim(a, at, size, 1)

    def rows(a, at, size):
        return lax.dynamic_slice_in_dim(a, at, size, 0)

    head_width = wq.shape[1] // 3
    bias3 = qkv_bias.reshape(3, head_width)
    mixed = jnp.stack(
        [
            dot(normed, wq[:, s * head_width : (s + 1) * head_width], nn) + bias3[s][None]
            for s in range(3)
        ]
    )
    context_grad = dot(cot, wd, nt).astype(BF)
    hidden_grad = dot(cot, w2, nt)
    hidden_pre = dot(normed, w1, nn) + fc1_bias.reshape(1, -1)
    hidden_f, pull = jax.vjp(lambda v: jax.nn.gelu(v, approximate=True), hidden_pre)
    hidden = hidden_f.astype(BF)
    pre_grad = pull(hidden_grad)[0].astype(BF)

    def pair_grads(make):
        mine, theirs = make(mine_at), make(theirs_at)
        mine_sum = reduce_dp(mine).astype(BF)
        theirs_sum = reduce_dp(theirs).astype(BF)
        return mine_sum, swap_row(theirs_sum)

    fc2_pieces = pair_grads(lambda at: dot(hidden, cols(cot, at, half_width), tn))
    fc1_pieces = pair_grads(lambda at: dot(cols(normed, at, half_width), pre_grad, tn))

    cos, sin = rotation_tables(positions)
    context, mixed_grad = attention(mixed, context_grad, cos, sin, segment_ids)

    dense_pieces = pair_grads(lambda at: dot(context, cols(cot, at, half_width), tn))
    qkv_pieces = pair_grads(lambda at: dot(cols(normed, at, half_width), mixed_grad, tn))

    def out_part(at):
        return dot(context, cols(wd, at, half_width), nn) + dot(hidden, cols(w2, at, half_width), nn)

    summed_out = scatter_group(out_part(mine_at), out_part(theirs_at))
    block_output = (
        block_input.astype(F32) + summed_out + dense_bias[None] + fc2_bias[None]
    ).astype(BF)

    def normed_part(at):
        return dot(mixed_grad, rows(wq, at, half_width), nt) + dot(
            pre_grad, rows(w1, at, half_width), nt
        )

    part_mine, part_theirs = normed_part(mine_at), normed_part(theirs_at)

    def feature_sums(part, at):
        scaled = part * cols(gain, at, half_width)
        centred = (cols(whole, at, half_width).astype(F32) - row_mean) * inv_std
        return jnp.stack([jnp.sum(scaled, axis=-1), jnp.sum(scaled * centred, axis=-1)])

    totals = feature_sums(part_mine, mine_at) + feature_sums(part_theirs, theirs_at)
    totals = totals + swap_row(totals)
    gathered = [
        lax.ppermute(totals, "col", [(i, (i + s) % n_col) for i in range(n_col)])
        for s in range(1, n_col)
    ]
    for g in gathered:
        totals = totals + g
    normed_grad = scatter_group(part_mine, part_theirs)
    scaled_here = (block_input.astype(F32) - row_mean) * inv_std
    scaled_grad = normed_grad * ln_gain.astype(F32)[None]
    cot_float = cotangent.astype(F32)
    input_grad = cot_float + inv_std * (
        scaled_grad
        - totals[0][:, None] / full_width
        - scaled_here * totals[1][:, None] / full_width
    )
    small = jnp.concatenate(
        [
            jnp.sum(mixed_grad.astype(F32), axis=0),
            jnp.sum(pre_grad.astype(F32), axis=0),
            jnp.sum(cot_float, axis=0),
            jnp.sum(normed_grad * scaled_here, axis=0),
            jnp.sum(normed_grad, axis=0),
        ]
    )
    small = sum_all_dp(small)
    n_mixed, n_pre = mixed_grad.shape[1], pre_grad.shape[1]
    qkv_bias_grad = small[:n_mixed].reshape(qkv_bias.shape)
    fc1_bias_grad = small[n_mixed : n_mixed + n_pre].reshape(fc1_bias.shape)
    at = n_mixed + n_pre
    bias_grad, gain_grad, shift_grad = (
        small[at + i * part_width : at + (i + 1) * part_width] for i in range(3)
    )

    order = spread_order()

    def assemble(pieces, place, shape):
        everyone = spread_dp(list(pieces))
        out = jnp.zeros(shape, F32)
        for m, ps in zip(order, everyone):
            q = jnp.bitwise_xor(d, m)
            for rr, piece in ((r, ps[0]), (1 - r, ps[1])):
                out = place(out, piece.astype(F32), q, rr)
        return out

    def put(out, piece, *at):
        return lax.dynamic_update_slice(out, piece, at)

    def place_in(out, piece, q, rr):
        m, w = piece.shape
        return put(out, piece, q * m, rr * w)

    def place_out(out, piece, q, rr):
        m, w = piece.shape
        return put(out, piece, rr * m * n_dp + q * m, 0)

    def place_qkv(out, piece, q, rr):
        m, w = piece.shape
        for s in range(3):
            out = put(
                out, piece[:, s * head_width : (s + 1) * head_width][None], s, q * m, rr * head_width
            )
        return out

    fc2_grad = assemble(fc2_pieces, place_out, fc2_weight.shape)
    fc1_grad = assemble(fc1_pieces, place_in, fc1_weight.shape)
    dense_grad = assemble(dense_pieces, place_out, dense_weight.shape)
    shape = (3, qkv_weight.shape[0], qkv_weight.shape[2])
    qkv_grad = jnp.transpose(assemble(qkv_pieces, place_qkv, shape), (1, 0, 2))
    return (
        block_output,
        input_grad,
        gain_grad,
        shift_grad,
        qkv_grad,
        qkv_bias_grad,
        dense_grad,
        bias_grad,
        fc1_grad,
        fc1_bias_grad,
        fc2_grad,
        bias_grad,
    )


def solution(mesh):
    return jax.shard_map(
        local,
        mesh=mesh,
        in_specs=(
            P("dp", ("row", "col")),
            P("dp"),
            P("dp"),
            P(("row", "col")),
            P(("row", "col")),
            P("row", None, "col"),
            P(None, "col", "row", None),
            P("col", "row"),
            P(("row", "col")),
            P("row", "col"),
            P("col", "row", None),
            P("col", "row"),
            P(("row", "col")),
            P("dp", ("row", "col")),
        ),
        out_specs=(
            P("dp", ("row", "col")),
            P("dp", ("row", "col")),
            P(("row", "col")),
            P(("row", "col")),
            P("row", None, "col"),
            P(None, "col", "row", None),
            P("col", "row"),
            P(("row", "col")),
            P("row", "col"),
            P("col", "row", None),
            P("col", "row"),
            P(("row", "col")),
        ),
        check_vma=False,
    )
```

time: 1300 us -> 568 us (0.44)
  waiting for transfers between devices: 935 us -> 162 us
  Pallas kernels: 0 us -> 156 us
  blocking collectives: 68.2 us -> 0 us
  starting transfers between devices: 1.42 us -> 61.8 us
  local copies, waits for them, and re-layouts: 84.2 us -> 49.4 us
  matrix products: 125 us -> 95.2 us
  other arithmetic: 49.8 us -> 36.8 us
    psum x1 -> x0, waiting for transfers between devices: 427 us -> none  [local(): lax.psum((gain_grad, shift_grad, qkv_grad, qkv_bias_grad, dense_grad, bia...]
    reduce_scatter x6 -> x0, waiting for transfers between devices: 323 us -> none  [the longest x1 102 us: local(): lax.psum_scatter(part_up, 'row', scatter_dimension=1, tiled=True)]
    all_gather x6 -> x0, waiting for transfers between devices: 183 us -> none  [the longest x1 51.2 us: local(): lax.all_gather(hidden, 'row', axis=1, tiled=True)]
    ppermute x0 -> x58, waiting for transfers between devices: none -> 162 us  [the longest x42 86.5 us: swap_dp(): return lax.ppermute(value, 'dp', [(i, i ^ 1 << bit) for i in range(n)])]
    pallas_call x0 -> x2, Pallas kernels: none -> 156 us  [the longest x1 130 us: gather_all(): pl.pallas_call(functools.partial(gather_kernel, n_col), out_shape=tuple((...]
    ppermute x0 -> x58, starting transfers between devices: none -> 61.8 us  [the longest x42 29.7 us: swap_dp(): return lax.ppermute(value, 'dp', [(i, i ^ 1 << bit) for i in range(n)])]
    all_gather x2 -> x0, blocking collectives: 34.8 us -> none  [the longest x1 17.9 us: local(): lax.all_gather(ln_gain, ('row', 'col'), axis=0, tiled=True)]
    psum x2 -> x0, blocking collectives: 33.4 us -> none  [the longest x1 21.9 us: local(): lax.psum((jnp.sum(scaled_grad, axis=-1), jnp.sum(scaled_grad * scaled_her...]
  transfers between devices with their start and end apart: 13 -> 58, of which waited for: 11 -> 22; matrix products, arithmetic and copies ran while one was open for 17% -> 20% of each run, Pallas kernels for 0% -> 0%
where the time goes in v1:
time: 568 us; the launch traced here: 564 us
  waiting for transfers between devices  162 us (29%)
  Pallas kernels  156 us (27%)
  matrix products  95.2 us (17%)
  starting transfers between devices  61.8 us (11%)
  local copies, waits for them, and re-layouts  49.4 us (9%)
  other arithmetic  36.8 us (6%)
    pallas_call x1, Pallas kernels, gather_all(): pl.pallas_call(functools.partial(gather_kernel, n_col), out_shape=tuple((...  130 us
    dot_general x22, matrix products, dot(): return lax.dot_general(a, b, (dims, ((), ())), preferred_element_type=F32)  95.2 us
    ppermute x42, waiting for transfers between devices, swap_dp(): return lax.ppermute(value, 'dp', [(i, i ^ 1 << bit) for i in range(n)])  86.5 us
    ppermute x6, waiting for transfers between devices, scatter_group(): lax.ppermute(chunk(s).astype(BF), 'col', [(i, (i + s) % n_col) for i in r...  61.5 us
    ppermute x42, starting transfers between devices, swap_dp(): return lax.ppermute(value, 'dp', [(i, i ^ 1 << bit) for i in range(n)])  29.7 us
    pallas_call x1, Pallas kernels, attention(): pl.pallas_call(functools.partial(attention_kernel, query_rows=min(QUERY_R...  25.5 us
    ppermute x6, starting transfers between devices, scatter_group(): lax.ppermute(chunk(s).astype(BF), 'col', [(i, (i + s) % n_col) for i in r...  19.5 us
    dynamic_update_slice x24, other arithmetic, put(): return lax.dynamic_update_slice(out, piece, at)  17.7 us
  transfers between devices with their start and end apart: 58, of which 22 were waited for; matrix products, arithmetic and copies ran while one was open for 20% of the time, Pallas kernels for 0%

profile of v1, /device:TPU:0, one launch (start us, length us, event | category | flops | bytes accessed | tf_op | source)
XLA Modules:
  0.0 563.7 jit_solution(1093693707045595198)
XLA Ops:
  3.0 2.2 copy-done.9
  9.4 130.4 %shard_map.229 = (bf16[1024,2048]{1,0:T(8,128)(2,1)S(1)}, bf16[1024,2048]{1,0:T(8,128)(2,1)S(1)}, f32[16,2048]{1,0:T(8,128)S(1)}, bf16[2048,768]{1,0:T(8,128)(2,...) custom-call(bf16[1024,256]{1,0:T(8,128)(2,1)S(1)} %copy-done.7, ...), custom_call_target="tpu_custom_call" | custom-call | bytes 314572800 | tf_op jit(solution)/shard_map/pallas_call | solution.py:307
  149.4 2.3 fusion.47
  151.7 2.2 fusion.48
  153.9 2.3 fusion.49
  157.2 10.1 %fusion.132 = f32[1024,1024]{1,0:T(8,128)} fusion(bf16[1024,2048]{1,0:T(8,128)(2,1)} %copy-done.28, bf16[2048,1024]{1,0:T(8,128)(2,1)} %copy-done.14), kind=kOutput, calls=%fused_computation.249 | convolution fusion | flops 4294967296 | bytes 12582912 | tf_op jit(solution)/shard_map/dot_general | solution.py:597
  173.2 2.3 concatenate.14.sin_ref
  175.6 3.4 pad_maximum_fusion.mixed_ref
  179.0 25.5 %shard_map.230 = (bf16[1024,256]{1,0:T(8,128)(2,1)}, bf16[1024,768]{1,0:T(8,128)(2,1)}) custom-call(f32[3,1024,256]{2,1,0:T(8,128)} %pad_maximum_fusion.mixed_ref, bf16[1024,256]{1,0:T(8,128)(2,1)} %convolution_convert_fusion.grad_ref, f32[1024,128]{1,0:T(8,128)} %concatenate.13.cos_ref, f32[1024,128]{1,0:T(8,128)} %concatenate.14.sin_ref, ...), custom_call_target="tpu_custom_call" | custom-call | flops 20000000000 | bytes 67108864 | tf_op jit(solution)/shard_map/pallas_call | solution.py:434
  204.5 3.4 fusion.43
  208.4 9.4 %convert_reduce_fusion.1 = (f32[1024]{0:T(1024)S(1)}, bf16[1024,1024]{1,0:T(8,128)(2,1)S(1)}, bf16[1024,1024]{1,0:T(8,128)(2,1)S(1)}) fusion(f32[1024,1024]{1,0:T(8,128)} %fusion.132, f32[1024]{0:T(1024)S(1)} %bitcast.276, bf16[1024,2048]{1,0:T(8,128)(2,1)S(1)} %copy-done.4, bf16[1024,2048]{1,0:T(8,128)(2,1)S(1)} %copy-done.18), kind=kOutput, calls=%fused_computation.17 | convolution fusion | flops 4321180672 | bytes 16785408 | tf_op jit(solution)/shard_map/dot_general | solution.py:597
  217.8 5.2 fusion.131
  224.5 2.3 fusion.17
  229.4 5.6 fusion.41
  235.0 2.4 fusion.67
  237.4 4.1 fusion.37
  245.8 3.9 fusion.45
  249.6 6.1 %fusion.19 = f32[1024,1024]{1,0:T(8,128)} fusion(bf16[1024,1024]{1,0:T(8,128)(2,1)S(1)} %get-tuple-element.47, bf16[1024,2048]{1,0:T(8,128)(2,1)} %copy-done.17, s32[]{:T(128)S(6)} %select_n.102), kind=kOutput, calls=%fused_computation.42 | convolution fusion | flops 2147483648 | bytes 8388612 | tf_op jit(solution)/shard_map/dot_general | solution.py:597
  257.5 3.5 fusion.33
  260.9 6.8 %fusion.39 = f32[1024,1024]{1,0:T(8,128)} fusion(bf16[1024,1024]{1,0:T(8,128)(2,1)} %copy-done.53, bf16[1024,2048]{1,0:T(8,128)(2,1)} %copy-done.28, s32[]{:T(128)S(6)} %select_n.102), kind=kOutput, calls=%fused_computation.58 | convolution fusion | flops 2147483648 | bytes 8388612 | tf_op jit(solution)/shard_map/dot_general | solution.py:597
  267.7 4.5 fusion.35
  272.2 4.4 fusion.31
  276.6 4.4 fusion.27
  280.9 2.9 fusion.60
  283.8 2.7 fusion.61
  286.6 2.7 fusion.62
  294.5 4.1 collective-permute-done.28
  300.2 3.5 collective-permute-done.26
  305.5 11.3 %collective-permute-done.29 = bf16[64,1024]{1,0:T(8,128)(2,1)S(1)} collective-permute-done((bf16[64,1024]{1,0:T(8,128)(2,1)S(1)}, bf16[64,1024]{1,0:T(8,128)(2,1)S(1)}, u32[]{:S(2)}, u32[]{:S(2)}) %collective-permute-start.29) | collective-permute-done | bytes 131104 | tf_op jit(solution)/shard_map/ppermute | solution.py:468
  318.4 4.6 collective-permute-done.30
  324.5 3.4 collective-permute-done.31
  342.9 6.5 %collective-permute-done.15 = bf16[1,256,768]{2,1,0:T(8,128)(2,1)S(1)} collective-permute-done((bf16[1,256,768]{2,1,0:T(8,128)(2,1)S(1)}, bf16[1,256,768]{2,1,0:T(8,128)(2,1)S(1)}, u32[]{:S(2)}, u32[]{:S(2)}) %collective-permute-start.15) | collective-permute-done | bytes 393248 | tf_op jit(solution)/shard_map/ppermute | solution.py:473
  351.9 5.9 %collective-permute-done.17 = bf16[1,256,768]{2,1,0:T(8,128)(2,1)S(1)} collective-permute-done((bf16[1,256,768]{2,1,0:T(8,128)(2,1)S(1)}, bf16[1,256,768]{2,1,0:T(8,128)(2,1)S(1)}, u32[]{:S(2)}, u32[]{:S(2)}) %collective-permute-start.17) | collective-permute-done | bytes 393248 | tf_op jit(solution)/shard_map/ppermute | solution.py:473
  359.4 20.9 %collective-permute-done.39 = bf16[1,256,1024]{2,1,0:T(8,128)(2,1)S(1)} collective-permute-done((bf16[1,256,1024]{2,1,0:T(8,128)(2,1)S(1)}, bf16[1,256,1024]{2,1,0:T(8,128)(2,1)S(1)}, u32[]{:S(2)}, u32[]{:S(2)}) %collective-permute-start.39) | collective-permute-done | bytes 524320 | tf_op jit(solution)/shard_map/ppermute | solution.py:473
  383.5 4.5 broadcast_in_dim.139
  389.2 13.1 %collective-permute-done.50 = bf16[1,256,1024]{2,1,0:T(8,128)(2,1)S(1)} collective-permute-done((bf16[1,256,1024]{2,1,0:T(8,128)(2,1)S(1)}, bf16[1,256,1024]{2,1,0:T(8,128)(2,1)S(1)}, u32[]{:S(2)}, u32[]{:S(2)}) %collective-permute-start.50) | collective-permute-done | bytes 524320 | tf_op jit(solution)/shard_map/ppermute | solution.py:473
  404.1 4.5 broadcast_in_dim.140
  414.8 7.9 %collective-permute-done.20 = bf16[256,768]{1,0:T(8,128)(2,1)S(1)} collective-permute-done((bf16[256,768]{1,0:T(8,128)(2,1)S(1)}, bf16[256,768]{1,0:T(8,128)(2,1)S(1)}, u32[]{:S(2)}, u32[]{:S(2)}) %collective-permute-start.20) | collective-permute-done | bytes 393248 | tf_op jit(solution)/shard_map/ppermute | solution.py:473
  428.6 7.5 %multiply_reduce_fusion = (f32[1024]{0:T(1024)S(1)}, f32[1024]{0:T(1024)S(1)}, f32[1024]{0:T(1024)S(1)}, f32[1024]{0:T(1024)S(1)}, f32[1024,1024]{1,0:T(8,128)S(1)}) fusion(f32[1024,1024]{1,0:T(8,128)} %get-tuple-element.73, bf16[1024,2048]{1,0:T(8,128)(2,1)S(1)} %copy-done.1, s32[]{:T(128)S(6)} %select_n.103, f32[1024]{0:T(1024)S(1)} %bitcast.271, ...), kind=kOutput, calls=%fused_computation.18 | convolution fusion | flops 2165305344 | bytes 23102976 | tf_op jit(solution)/shard_map/dot_general | solution.py:597
  440.2 3.5 collective-permute-start.7
  444.7 2.4 convert_add_fusion.1
  451.6 3.1 collective-permute-done.11
  456.3 3.3 collective-permute-start.5
  459.6 8.3 %collective-permute-start.3 = (bf16[1024,256]{1,0:T(8,128)(2,1)S(1)}, bf16[1024,256]{1,0:T(8,128)(2,1)S(1)}, u32[]{:S(2)}, u32[]{:S(2)}) collective-permute-start(bf16[1024,256]{1,0:T(8,128)(2,1)S(1)} %get-tuple-element.53), channel_id=1, source_target_pairs={{0,3},{1,0},{2,1},{3,2},{4,7},{5,4},{6,5},{7,6},{8,11},{9,8},{10,9... | collective-permute-start | bytes 1572872 | tf_op jit(solution)/shard_map/ppermute | solution.py:531
  468.7 2.2 collective-permute-start.1
  471.0 43.5 %collective-permute-done.6 = bf16[1024,256]{1,0:T(8,128)(2,1)S(1)} collective-permute-done((bf16[1024,256]{1,0:T(8,128)(2,1)S(1)}, bf16[1024,256]{1,0:T(8,128)(2,1)S(1)}, u32[]{:S(2)}, u32[]{:S(2)}) %collective-permute-start.6) | collective-permute-done | bytes 524320 | tf_op jit(solution)/shard_map/ppermute | solution.py:531
  517.1 18.0 %collective-permute-done.2 = bf16[1024,256]{1,0:T(8,128)(2,1)S(1)} collective-permute-done((bf16[1024,256]{1,0:T(8,128)(2,1)S(1)}, bf16[1024,256]{1,0:T(8,128)(2,1)S(1)}, u32[]{:S(2)}, u32[]{:S(2)}) %collective-permute-start.2) | collective-permute-done | bytes 524320 | tf_op jit(solution)/shard_map/ppermute | solution.py:531
  544.1 7.4 %collective-permute-done.53 = bf16[256,1024]{1,0:T(8,128)(2,1)S(1)} collective-permute-done((bf16[256,1024]{1,0:T(8,128)(2,1)S(1)}, bf16[256,1024]{1,0:T(8,128)(2,1)S(1)}, u32[]{:S(2)}, u32[]{:S(2)}) %collective-permute-start.53) | collective-permute-done | bytes 524320 | tf_op jit(solution)/shard_map/ppermute | solution.py:473
  (333 shorter events, 117.3 us)
Async XLA Ops:
  223.0 205.0 %collective-permute-start.4 = (bf16[1024,1024]{1,0:T(8,128)(2,1)}, bf16[1024,1024]{1,0:T(8,128)(2,1)}, u32[]{:S(2)}, u32[]{:S(2)}) collective-permute-start(bf16[1024,1024]{1,0:T(8,128)(2,1)} %get-tuple-element.72), channel_id=1, source_target_pairs={{0,4},{4,0},{1,5},{5,1},{2,6},{6,2},{3,7},{7,3},{8,12},{12,8},{9,1... | collective-permute-start | bytes 6291464 | tf_op jit(solution)/shard_map/ppermute | solution.py:468
  228.9 215.8 %collective-permute-start = (bf16[1024,1024]{1,0:T(8,128)(2,1)}, bf16[1024,1024]{1,0:T(8,128)(2,1)}, u32[]{:S(2)}, u32[]{:S(2)}) collective-permute-start(bf16[1024,1024]{1,0:T(8,128)(2,1)} %add_convert_fusion), channel_id=1, source_target_pairs={{0,4},{4,0},{1,5},{5,1},{2,6},{6,2},{3,7},{7,3},{8,12},{12,8},{9,1... | collective-permute-start | bytes 6291464 | tf_op jit(solution)/shard_map/ppermute | solution.py:468
  237.4 94.8 %collective-permute-start.14 = (bf16[2,256,768]{2,1,0:T(8,128)(2,1)}, bf16[2,256,768]{2,1,0:T(8,128)(2,1)}, u32[]{:S(2)}, u32[]{:S(2)}) collective-permute-start(bf16[2,256,768]{2,1,0:T(8,128)(2,1)} %fusion.67), channel_id=1, source_target_pairs={{0,8},{8,0},{16,24},{24,16},{1,9},{9,1},{17,25},{25,17},{2,10},{10... | collective-permute-start | bytes 2359304 | tf_op jit(solution)/shard_map/ppermute | solution.py:473
  242.5 91.7 %collective-permute-start.16 = (bf16[2,256,768]{2,1,0:T(8,128)(2,1)}, bf16[2,256,768]{2,1,0:T(8,128)(2,1)}, u32[]{:S(2)}, u32[]{:S(2)}) collective-permute-start(bf16[2,256,768]{2,1,0:T(8,128)(2,1)} %fusion.68), channel_id=1, source_target_pairs={{0,8},{8,0},{16,24},{24,16},{1,9},{9,1},{17,25},{25,17},{2,10},{10... | collective-permute-start | bytes 2359304 | tf_op jit(solution)/shard_map/ppermute | solution.py:473
  245.3 46.0 %collective-permute-start.27 = (bf16[2,64,1024]{2,1,0:T(8,128)(2,1)}, bf16[2,64,1024]{2,1,0:T(8,128)(2,1)S(1)}, u32[]{:S(2)}, u32[]{:S(2)}) collective-permute-start(bf16[2,64,1024]{2,1,0:T(8,128)(2,1)} %fusion.78), channel_id=1, source_target_pairs={{0,8},{8,0},{16,24},{24,16},{1,9},{9,1},{17,25},{25,17},{2,10},{10... | collective-permute-start | bytes 786440 | tf_op jit(solution)/shard_map/ppermute | solution.py:473
  292.9 5.8 %collective-permute-start.28 = (bf16[1,64,1024]{2,1,0:T(8,128)(2,1)S(1)}, bf16[1,64,1024]{2,1,0:T(8,128)(2,1)S(1)}, u32[]{:S(2)}, u32[]{:S(2)}) collective-permute-start(bf16[1,64,1024]{2,1,0:T(8,128)(2,1)S(1)} %dynamic-slice_convert_fusion.12), channel_id=1, source_target_pairs={{0,16},{8,24},{16,0},{24,8},{1,17},{9,25},{17,1},{25,9},{2,18},{10... | collective-permute-start | bytes 393224 | tf_op jit(solution)/shard_map/ppermute | solution.py:473
  298.7 5.1 collective-permute-start.26
  303.7 13.1 %collective-permute-start.29 = (bf16[64,1024]{1,0:T(8,128)(2,1)S(1)}, bf16[64,1024]{1,0:T(8,128)(2,1)S(1)}, u32[]{:S(2)}, u32[]{:S(2)}) collective-permute-start(bf16[64,1024]{1,0:T(8,128)(2,1)S(1)} %fusion.104), channel_id=1, source_target_pairs={{0,4},{4,0},{1,5},{5,1},{2,6},{6,2},{3,7},{7,3},{8,12},{12,8},{9,1... | collective-permute-start | bytes 393224 | tf_op jit(solution)/shard_map/ppermute | solution.py:468
  316.8 6.1 %collective-permute-start.30 = (bf16[64,1024]{1,0:T(8,128)(2,1)S(1)}, bf16[64,1024]{1,0:T(8,128)(2,1)S(1)}, u32[]{:S(2)}, u32[]{:S(2)}) collective-permute-start(bf16[64,1024]{1,0:T(8,128)(2,1)S(1)} %get-tuple-element.41), channel_id=1, source_target_pairs={{0,16},{8,24},{16,0},{24,8},{1,17},{9,25},{17,1},{25,9},{2,18},{10... | collective-permute-start | bytes 393224 | tf_op jit(solution)/shard_map/ppermute | solution.py:473
  322.9 5.0 collective-permute-start.31
  332.2 5.2 collective-permute-start.38
  337.4 12.0 %collective-permute-start.15 = (bf16[1,256,768]{2,1,0:T(8,128)(2,1)S(1)}, bf16[1,256,768]{2,1,0:T(8,128)(2,1)S(1)}, u32[]{:S(2)}, u32[]{:S(2)}) collective-permute-start(bf16[1,256,768]{2,1,0:T(8,128)(2,1)S(1)} %dynamic-slice_convert_fusion.11), channel_id=1, source_target_pairs={{0,16},{8,24},{16,0},{24,8},{1,17},{9,25},{17,1},{25,9},{2,18},{10... | collective-permute-start | bytes 1179656 | tf_op jit(solution)/shard_map/ppermute | solution.py:473
  339.5 18.3 %collective-permute-start.17 = (bf16[1,256,768]{2,1,0:T(8,128)(2,1)S(1)}, bf16[1,256,768]{2,1,0:T(8,128)(2,1)S(1)}, u32[]{:S(2)}, u32[]{:S(2)}) collective-permute-start(bf16[1,256,768]{2,1,0:T(8,128)(2,1)S(1)} %dynamic-slice_convert_fusion.10), channel_id=1, source_target_pairs={{0,16},{8,24},{16,0},{24,8},{1,17},{9,25},{17,1},{25,9},{2,18},{10... | collective-permute-start | bytes 1179656 | tf_op jit(solution)/shard_map/ppermute | solution.py:473
  341.5 40.5 %collective-permute-start.37 = (bf16[1,256,1024]{2,1,0:T(8,128)(2,1)S(1)}, bf16[1,256,1024]{2,1,0:T(8,128)(2,1)S(1)}, u32[]{:S(2)}, u32[]{:S(2)}) collective-permute-start(bf16[1,256,1024]{2,1,0:T(8,128)(2,1)S(1)} %dynamic-slice_convert_fusion.3), channel_id=1, source_target_pairs={{0,16},{8,24},{16,0},{24,8},{1,17},{9,25},{17,1},{25,9},{2,18},{10... | collective-permute-start | bytes 1572872 | tf_op jit(solution)/shard_map/ppermute | solution.py:473
  349.4 30.9 %collective-permute-start.39 = (bf16[1,256,1024]{2,1,0:T(8,128)(2,1)S(1)}, bf16[1,256,1024]{2,1,0:T(8,128)(2,1)S(1)}, u32[]{:S(2)}, u32[]{:S(2)}) collective-permute-start(bf16[1,256,1024]{2,1,0:T(8,128)(2,1)S(1)} %dynamic-slice_convert_fusion.2), channel_id=1, source_target_pairs={{0,16},{8,24},{16,0},{24,8},{1,17},{9,25},{17,1},{25,9},{2,18},{10... | collective-permute-start | bytes 1572872 | tf_op jit(solution)/shard_map/ppermute | solution.py:473
  357.8 46.1 %collective-permute-start.48 = (bf16[1,256,1024]{2,1,0:T(8,128)(2,1)S(1)}, bf16[1,256,1024]{2,1,0:T(8,128)(2,1)S(1)}, u32[]{:S(2)}, u32[]{:S(2)}) collective-permute-start(bf16[1,256,1024]{2,1,0:T(8,128)(2,1)S(1)} %dynamic-slice_convert_fusion.1), channel_id=1, source_target_pairs={{0,16},{8,24},{16,0},{24,8},{1,17},{9,25},{17,1},{25,9},{2,18},{10... | collective-permute-start | bytes 1572872 | tf_op jit(solution)/shard_map/ppermute | solution.py:473
  380.3 22.0 %collective-permute-start.50 = (bf16[1,256,1024]{2,1,0:T(8,128)(2,1)S(1)}, bf16[1,256,1024]{2,1,0:T(8,128)(2,1)S(1)}, u32[]{:S(2)}, u32[]{:S(2)}) collective-permute-start(bf16[1,256,1024]{2,1,0:T(8,128)(2,1)S(1)} %dynamic-slice_convert_fusion), channel_id=1, source_target_pairs={{0,16},{8,24},{16,0},{24,8},{1,17},{9,25},{17,1},{25,9},{2,18},{10... | collective-permute-start | bytes 1572872 | tf_op jit(solution)/shard_map/ppermute | solution.py:473
  382.0 27.7 %collective-permute-start.18 = (bf16[256,768]{1,0:T(8,128)(2,1)S(1)}, bf16[256,768]{1,0:T(8,128)(2,1)S(1)}, u32[]{:S(2)}, u32[]{:S(2)}) collective-permute-start(bf16[256,768]{1,0:T(8,128)(2,1)S(1)} %fusion.76), channel_id=1, source_target_pairs={{0,4},{4,0},{1,5},{5,1},{2,6},{6,2},{3,7},{7,3},{8,12},{12,8},{9,1... | collective-permute-start | bytes 1179656 | tf_op jit(solution)/shard_map/ppermute | solution.py:468
  402.3 10.7 %collective-permute-start.19 = (bf16[256,768]{1,0:T(8,128)(2,1)S(1)}, bf16[256,768]{1,0:T(8,128)(2,1)S(1)}, u32[]{:S(2)}, u32[]{:S(2)}) collective-permute-start(bf16[256,768]{1,0:T(8,128)(2,1)S(1)} %get-tuple-element.43), channel_id=1, source_target_pairs={{0,16},{8,24},{16,0},{24,8},{1,17},{9,25},{17,1},{25,9},{2,18},{10... | collective-permute-start | bytes 1179656 | tf_op jit(solution)/shard_map/ppermute | solution.py:473
  404.0 10.6 %collective-permute-start.21 = (bf16[256,768]{1,0:T(8,128)(2,1)S(1)}, bf16[256,768]{1,0:T(8,128)(2,1)S(1)}, u32[]{:S(2)}, u32[]{:S(2)}) collective-permute-start(bf16[256,768]{1,0:T(8,128)(2,1)S(1)} %get-tuple-element.43), channel_id=1, source_target_pairs={{0,8},{8,0},{16,24},{24,16},{1,9},{9,1},{17,25},{25,17},{2,10},{10... | collective-permute-start | bytes 1179656 | tf_op jit(solution)/shard_map/ppermute | solution.py:473
  409.7 26.8 %collective-permute-start.40 = (bf16[256,1024]{1,0:T(8,128)(2,1)S(1)}, bf16[256,1024]{1,0:T(8,128)(2,1)S(1)}, u32[]{:S(2)}, u32[]{:S(2)}) collective-permute-start(bf16[256,1024]{1,0:T(8,128)(2,1)S(1)} %fusion.70), channel_id=1, source_target_pairs={{0,4},{4,0},{1,5},{5,1},{2,6},{6,2},{3,7},{7,3},{8,12},{12,8},{9,1... | collective-permute-start | bytes 1572872 | tf_op jit(solution)/shard_map/ppermute | solution.py:468
  412.9 9.8 %collective-permute-start.20 = (bf16[256,768]{1,0:T(8,128)(2,1)S(1)}, bf16[256,768]{1,0:T(8,128)(2,1)S(1)}, u32[]{:S(2)}, u32[]{:S(2)}) collective-permute-start(bf16[256,768]{1,0:T(8,128)(2,1)S(1)} %collective-permute-done.18), channel_id=1, source_target_pairs={{0,16},{8,24},{16,0},{24,8},{1,17},{9,25},{17,1},{25,9},{2,18},{10... | collective-permute-start | bytes 1179656 | tf_op jit(solution)/shard_map/ppermute | solution.py:473
  414.6 9.7 %collective-permute-start.22 = (bf16[256,768]{1,0:T(8,128)(2,1)S(1)}, bf16[256,768]{1,0:T(8,128)(2,1)S(1)}, u32[]{:S(2)}, u32[]{:S(2)}) collective-permute-start(bf16[256,768]{1,0:T(8,128)(2,1)S(1)} %collective-permute-done.18), channel_id=1, source_target_pairs={{0,8},{8,0},{16,24},{24,16},{1,9},{9,1},{17,25},{25,17},{2,10},{10... | collective-permute-start | bytes 1179656 | tf_op jit(solution)/shard_map/ppermute | solution.py:473
  422.7 14.9 %collective-permute-start.41 = (bf16[256,1024]{1,0:T(8,128)(2,1)S(1)}, bf16[256,1024]{1,0:T(8,128)(2,1)S(1)}, u32[]{:S(2)}, u32[]{:S(2)}) collective-permute-start(bf16[256,1024]{1,0:T(8,128)(2,1)S(1)} %get-tuple-element.39), channel_id=1, source_target_pairs={{0,16},{8,24},{16,0},{24,8},{1,17},{9,25},{17,1},{25,9},{2,18},{10... | collective-permute-start | bytes 1572872 | tf_op jit(solution)/shard_map/ppermute | solution.py:473
  426.1 14.0 %collective-permute-start.51 = (bf16[256,1024]{1,0:T(8,128)(2,1)S(1)}, bf16[256,1024]{1,0:T(8,128)(2,1)S(1)}, u32[]{:S(2)}, u32[]{:S(2)}) collective-permute-start(bf16[256,1024]{1,0:T(8,128)(2,1)S(1)} %fusion.72), channel_id=1, source_target_pairs={{0,4},{4,0},{1,5},{5,1},{2,6},{6,2},{3,7},{7,3},{8,12},{12,8},{9,1... | collective-permute-start | bytes 1572872 | tf_op jit(solution)/shard_map/ppermute | solution.py:468
  428.0 19.1 %collective-permute-start.52 = (bf16[256,1024]{1,0:T(8,128)(2,1)S(1)}, bf16[256,1024]{1,0:T(8,128)(2,1)S(1)}, u32[]{:S(2)}, u32[]{:S(2)}) collective-permute-start(bf16[256,1024]{1,0:T(8,128)(2,1)S(1)} %get-tuple-element.37), channel_id=1, source_target_pairs={{0,16},{8,24},{16,0},{24,8},{1,17},{9,25},{17,1},{25,9},{2,18},{10... | collective-permute-start | bytes 1572872 | tf_op jit(solution)/shard_map/ppermute | solution.py:473
  436.4 31.5 %collective-permute-start.24 = (bf16[256,768]{1,0:T(8,128)(2,1)S(1)}, bf16[256,768]{1,0:T(8,128)(2,1)S(1)}, u32[]{:S(2)}, u32[]{:S(2)}) collective-permute-start(bf16[256,768]{1,0:T(8,128)(2,1)S(1)} %collective-permute-done.20), channel_id=1, source_target_pairs={{0,8},{8,0},{16,24},{24,16},{1,9},{9,1},{17,25},{25,17},{2,10},{10... | collective-permute-start | bytes 1179656 | tf_op jit(solution)/shard_map/ppermute | solution.py:473
  437.6 10.6 %collective-permute-start.8 = (f32[2,1024]{1,0:T(2,128)S(1)}, f32[2,1024]{1,0:T(2,128)S(1)}, u32[]{:S(2)}, u32[]{:S(2)}) collective-permute-start(f32[2,1024]{1,0:T(2,128)S(1)} %maximum_add_fusion), channel_id=1, source_target_pairs={{0,4},{4,0},{1,5},{5,1},{2,6},{6,2},{3,7},{7,3},{8,12},{12,8},{9,1... | collective-permute-start | bytes 24584 | tf_op jit(solution)/shard_map/ppermute | solution.py:468
  440.2 28.6 %collective-permute-start.7 = (bf16[1024,256]{1,0:T(8,128)(2,1)S(1)}, bf16[1024,256]{1,0:T(8,128)(2,1)S(1)}, u32[]{:S(2)}, u32[]{:S(2)}) collective-permute-start(bf16[1024,256]{1,0:T(8,128)(2,1)S(1)} %get-tuple-element.50), channel_id=1, source_target_pairs={{0,3},{1,0},{2,1},{3,2},{4,7},{5,4},{6,5},{7,6},{8,11},{9,8},{10,9... | collective-permute-start | bytes 1572872 | tf_op jit(solution)/shard_map/ppermute | solution.py:531
  448.3 6.5 %collective-permute-start.11 = (f32[2,1024]{1,0:T(2,128)S(1)}, f32[2,1024]{1,0:T(2,128)S(1)}, u32[]{:S(2)}, u32[]{:S(2)}) collective-permute-start(f32[2,1024]{1,0:T(2,128)S(1)} %fusion.158), channel_id=1, source_target_pairs={{0,3},{1,0},{2,1},{3,2},{4,7},{5,4},{6,5},{7,6},{8,11},{9,8},{10,9... | collective-permute-start | bytes 24584 | tf_op jit(solution)/shard_map/ppermute | solution.py:662
  450.3 6.1 %collective-permute-start.10 = (f32[2,1024]{1,0:T(2,128)S(1)}, f32[2,1024]{1,0:T(2,128)S(1)}, u32[]{:S(2)}, u32[]{:S(2)}) collective-permute-start(f32[2,1024]{1,0:T(2,128)S(1)} %fusion.158), channel_id=1, source_target_pairs={{0,2},{1,3},{2,0},{3,1},{4,6},{5,7},{6,4},{7,5},{8,10},{9,11},{10,... | collective-permute-start | bytes 24584 | tf_op jit(solution)/shard_map/ppermute | solution.py:662
  450.3 9.4 %collective-permute-start.9 = (f32[2,1024]{1,0:T(2,128)S(1)}, f32[2,1024]{1,0:T(2,128)S(1)}, u32[]{:S(2)}, u32[]{:S(2)}) collective-permute-start(f32[2,1024]{1,0:T(2,128)S(1)} %fusion.158), channel_id=1, source_target_pairs={{0,1},{1,2},{2,3},{3,0},{4,5},{5,6},{6,7},{7,4},{8,9},{9,10},{10,1... | collective-permute-start | bytes 24584 | tf_op jit(solution)/shard_map/ppermute | solution.py:662
  454.7 59.8 %collective-permute-start.6 = (bf16[1024,256]{1,0:T(8,128)(2,1)S(1)}, bf16[1024,256]{1,0:T(8,128)(2,1)S(1)}, u32[]{:S(2)}, u32[]{:S(2)}) collective-permute-start(bf16[1024,256]{1,0:T(8,128)(2,1)S(1)} %get-tuple-element.51), channel_id=1, source_target_pairs={{0,2},{1,3},{2,0},{3,1},{4,6},{5,7},{6,4},{7,5},{8,10},{9,11},{10,... | collective-permute-start | bytes 1572872 | tf_op jit(solution)/shard_map/ppermute | solution.py:531
  456.3 58.1 %collective-permute-start.5 = (bf16[1024,256]{1,0:T(8,128)(2,1)S(1)}, bf16[1024,256]{1,0:T(8,128)(2,1)S(1)}, u32[]{:S(2)}, u32[]{:S(2)}) collective-permute-start(bf16[1024,256]{1,0:T(8,128)(2,1)S(1)} %get-tuple-element.49), channel_id=1, source_target_pairs={{0,1},{1,2},{2,3},{3,0},{4,5},{5,6},{6,7},{7,4},{8,9},{9,10},{10,1... | collective-permute-start | bytes 1572872 | tf_op jit(solution)/shard_map/ppermute | solution.py:531
  459.6 55.9 %collective-permute-start.3 = (bf16[1024,256]{1,0:T(8,128)(2,1)S(1)}, bf16[1024,256]{1,0:T(8,128)(2,1)S(1)}, u32[]{:S(2)}, u32[]{:S(2)}) collective-permute-start(bf16[1024,256]{1,0:T(8,128)(2,1)S(1)} %get-tuple-element.53), channel_id=1, source_target_pairs={{0,3},{1,0},{2,1},{3,2},{4,7},{5,4},{6,5},{7,6},{8,11},{9,8},{10,9... | collective-permute-start | bytes 1572872 | tf_op jit(solution)/shard_map/ppermute | solution.py:531
  468.0 67.2 %collective-permute-start.2 = (bf16[1024,256]{1,0:T(8,128)(2,1)S(1)}, bf16[1024,256]{1,0:T(8,128)(2,1)S(1)}, u32[]{:S(2)}, u32[]{:S(2)}) collective-permute-start(bf16[1024,256]{1,0:T(8,128)(2,1)S(1)} %get-tuple-element.54), channel_id=1, source_target_pairs={{0,2},{1,3},{2,0},{3,1},{4,6},{5,7},{6,4},{7,5},{8,10},{9,11},{10,... | collective-permute-start | bytes 1572872 | tf_op jit(solution)/shard_map/ppermute | solution.py:531
  468.7 66.4 %collective-permute-start.1 = (bf16[1024,256]{1,0:T(8,128)(2,1)S(1)}, bf16[1024,256]{1,0:T(8,128)(2,1)S(1)}, u32[]{:S(2)}, u32[]{:S(2)}) collective-permute-start(bf16[1024,256]{1,0:T(8,128)(2,1)S(1)} %get-tuple-element.52), channel_id=1, source_target_pairs={{0,1},{1,2},{2,3},{3,0},{4,5},{5,6},{6,7},{7,4},{8,9},{9,10},{10,1... | collective-permute-start | bytes 1572872 | tf_op jit(solution)/shard_map/ppermute | solution.py:531
  514.5 25.9 %collective-permute-start.43 = (bf16[256,1024]{1,0:T(8,128)(2,1)S(1)}, bf16[256,1024]{1,0:T(8,128)(2,1)S(1)}, u32[]{:S(2)}, u32[]{:S(2)}) collective-permute-start(bf16[256,1024]{1,0:T(8,128)(2,1)S(1)} %get-tuple-element.39), channel_id=1, source_target_pairs={{0,8},{8,0},{16,24},{24,16},{1,9},{9,1},{17,25},{25,17},{2,10},{10... | collective-permute-start | bytes 1572872 | tf_op jit(solution)/shard_map/ppermute | solution.py:473
  514.5 38.1 %collective-permute-start.54 = (bf16[256,1024]{1,0:T(8,128)(2,1)S(1)}, bf16[256,1024]{1,0:T(8,128)(2,1)S(1)}, u32[]{:S(2)}, u32[]{:S(2)}) collective-permute-start(bf16[256,1024]{1,0:T(8,128)(2,1)S(1)} %get-tuple-element.37), channel_id=1, source_target_pairs={{0,8},{8,0},{16,24},{24,16},{1,9},{9,1},{17,25},{25,17},{2,10},{10... | collective-permute-start | bytes 1572872 | tf_op jit(solution)/shard_map/ppermute | solution.py:473
  515.5 22.1 %collective-permute-start.42 = (bf16[256,1024]{1,0:T(8,128)(2,1)S(1)}, bf16[256,1024]{1,0:T(8,128)(2,1)S(1)}, u32[]{:S(2)}, u32[]{:S(2)}) collective-permute-start(bf16[256,1024]{1,0:T(8,128)(2,1)S(1)} %collective-permute-done.40), channel_id=1, source_target_pairs={{0,16},{8,24},{16,0},{24,8},{1,17},{9,25},{17,1},{25,9},{2,18},{10... | collective-permute-start | bytes 1572872 | tf_op jit(solution)/shard_map/ppermute | solution.py:473
  535.2 6.3 %collective-permute-start.44 = (bf16[256,1024]{1,0:T(8,128)(2,1)S(1)}, bf16[256,1024]{1,0:T(8,128)(2,1)S(1)}, u32[]{:S(2)}, u32[]{:S(2)}) collective-permute-start(bf16[256,1024]{1,0:T(8,128)(2,1)S(1)} %collective-permute-done.40), channel_id=1, source_target_pairs={{0,8},{8,0},{16,24},{24,16},{1,9},{9,1},{17,25},{25,17},{2,10},{10... | collective-permute-start | bytes 1572872 | tf_op jit(solution)/shard_map/ppermute | solution.py:473
  535.2 7.9 %collective-permute-start.45 = (bf16[256,1024]{1,0:T(8,128)(2,1)S(1)}, bf16[256,1024]{1,0:T(8,128)(2,1)S(1)}, u32[]{:S(2)}, u32[]{:S(2)}) collective-permute-start(bf16[256,1024]{1,0:T(8,128)(2,1)S(1)} %collective-permute-done.41), channel_id=1, source_target_pairs={{0,8},{8,0},{16,24},{24,16},{1,9},{9,1},{17,25},{25,17},{2,10},{10... | collective-permute-start | bytes 1572872 | tf_op jit(solution)/shard_map/ppermute | solution.py:473
  537.6 13.9 %collective-permute-start.53 = (bf16[256,1024]{1,0:T(8,128)(2,1)S(1)}, bf16[256,1024]{1,0:T(8,128)(2,1)S(1)}, u32[]{:S(2)}, u32[]{:S(2)}) collective-permute-start(bf16[256,1024]{1,0:T(8,128)(2,1)S(1)} %collective-permute-done.51), channel_id=1, source_target_pairs={{0,16},{8,24},{16,0},{24,8},{1,17},{9,25},{17,1},{25,9},{2,18},{10... | collective-permute-start | bytes 1572872 | tf_op jit(solution)/shard_map/ppermute | solution.py:473
  540.4 13.9 %collective-permute-start.55 = (bf16[256,1024]{1,0:T(8,128)(2,1)S(1)}, bf16[256,1024]{1,0:T(8,128)(2,1)S(1)}, u32[]{:S(2)}, u32[]{:S(2)}) collective-permute-start(bf16[256,1024]{1,0:T(8,128)(2,1)S(1)} %collective-permute-done.51), channel_id=1, source_target_pairs={{0,8},{8,0},{16,24},{24,16},{1,9},{9,1},{17,25},{25,17},{2,10},{10... | collective-permute-start | bytes 1572872 | tf_op jit(solution)/shard_map/ppermute | solution.py:473
  541.5 15.5 %collective-permute-start.56 = (bf16[256,1024]{1,0:T(8,128)(2,1)S(1)}, bf16[256,1024]{1,0:T(8,128)(2,1)S(1)}, u32[]{:S(2)}, u32[]{:S(2)}) collective-permute-start(bf16[256,1024]{1,0:T(8,128)(2,1)S(1)} %collective-permute-done.52), channel_id=1, source_target_pairs={{0,8},{8,0},{16,24},{24,16},{1,9},{9,1},{17,25},{25,17},{2,10},{10... | collective-permute-start | bytes 1572872 | tf_op jit(solution)/shard_map/ppermute | solution.py:473
  543.0 12.3 %collective-permute-start.12 = (f32[2560]{0:T(1024)S(1)}, f32[2560]{0:T(1024)S(1)}, u32[]{:S(2)}, u32[]{:S(2)}) collective-permute-start(f32[2560]{0:T(1024)S(1)} %constant_dynamic-update-slice_fusion), channel_id=1, source_target_pairs={{0,8},{8,0},{16,24},{24,16},{1,9},{9,1},{17,25},{25,17},{2,10},{10... | collective-permute-start | bytes 30728 | tf_op jit(solution)/shard_map/ppermute | solution.py:473
  551.5 9.2 %collective-permute-start.46 = (bf16[256,1024]{1,0:T(8,128)(2,1)S(1)}, bf16[256,1024]{1,0:T(8,128)(2,1)S(1)}, u32[]{:S(2)}, u32[]{:S(2)}) collective-permute-start(bf16[256,1024]{1,0:T(8,128)(2,1)S(1)} %collective-permute-done.42), channel_id=1, source_target_pairs={{0,8},{8,0},{16,24},{24,16},{1,9},{9,1},{17,25},{25,17},{2,10},{10... | collective-permute-start | bytes 1572872 | tf_op jit(solution)/shard_map/ppermute | solution.py:473
  552.6 9.2 %collective-permute-start.57 = (bf16[256,1024]{1,0:T(8,128)(2,1)S(1)}, bf16[256,1024]{1,0:T(8,128)(2,1)S(1)}, u32[]{:S(2)}, u32[]{:S(2)}) collective-permute-start(bf16[256,1024]{1,0:T(8,128)(2,1)S(1)} %collective-permute-done.53), channel_id=1, source_target_pairs={{0,8},{8,0},{16,24},{24,16},{1,9},{9,1},{17,25},{25,17},{2,10},{10... | collective-permute-start | bytes 1572872 | tf_op jit(solution)/shard_map/ppermute | solution.py:473
  (65 other events, 788.8 us)

commit v2 on v0

v2 whole, which is shorter than its diff:
```python
import functools
import math

import jax
import jax.numpy as jnp
import numpy as np
from jax import lax
from jax.experimental import pallas as pl
from jax.experimental.pallas import tpu as pltpu
from jax.sharding import PartitionSpec as P

HEAD_DIM = 64
ROT_DIM = 32
NORM_EPSILON = 1e-05
MASKED_SCORE = -1e30
BLOCK = 256
MESH = pl.DeviceIdType.MESH
BF = jnp.bfloat16
F32 = jnp.float32
GELU_A = math.sqrt(2.0 / math.pi)
GELU_B = 0.044715
NN = (((1,), (0,)), ((), ()))
NT = (((1,), (1,)), ((), ()))
TN = (((0,), (0,)), ((), ()))


def dot(a, b, dims):
    return lax.dot_general(a, b, dims, preferred_element_type=F32)


def kernel(n_dp, n_col, *refs):
    names = (
        "x", "cot", "wq", "w1", "w2", "wd", "gb", "places", "seg_row", "freq", "qkv_bias",
        "fc1_bias", "out_bias", "gain_own", "y_out", "in_grad", "small", "f1", "f2", "fd", "fq",
        "rb1", "rb2", "rbd", "rbq", "rzo", "rzn", "xf", "cf", "gf", "wqf", "w1f",
        "w2f", "wdf", "normed", "hidden", "pg", "q", "k", "v", "dk", "dv", "bias", "cos", "sin",
        "ctx", "dctx", "mg", "lse", "g1", "g2", "gd", "gq", "stage1", "staged", "stageq", "stagez",
        "mean", "rstd", "tot", "small_v", "small_r", "x_send", "x_recv", "g_send", "g_recv",
        "c_send", "c_recv", "cx_send", "cx_recv", "w_send", "w_recv", "y_send", "y_recv",
        "s_send", "s_recv", "load_sem", "rs_send", "rs_recv", "xs_send", "xs_recv", "ag_send", "ag_recv", "part_sem",
        "stage_sem", "ox_send", "ox_recv", "oz_send", "oz_recv", "tot_send", "tot_recv", "sm_send",
        "sm_recv", "free_sem",
    )
    ns = dict(zip(names, refs, strict=True))
    (x_ref, cot_ref, wq_ref, w1_ref, w2_ref, wd_ref, gb_ref) = refs[:7]
    xf, cf, gf = ns["xf"], ns["cf"], ns["gf"]
    wqf, w1f, w2f, wdf = ns["wqf"], ns["w1f"], ns["w2f"], ns["wdf"]
    normed, hidden, pg = ns["normed"], ns["hidden"], ns["pg"]
    q_s, k_s, v_s, dk_s, dv_s = (ns[n] for n in ("q", "k", "v", "dk", "dv"))
    ctx, dctx, mg, lse = ns["ctx"], ns["dctx"], ns["mg"], ns["lse"]
    cos_ref, sin_ref, bias_s = ns["cos"], ns["sin"], ns["bias"]
    load_sem, stage_sem = ns["load_sem"], ns["stage_sem"]

    d = lax.axis_index("dp")
    r = lax.axis_index("row")
    c = lax.axis_index("col")
    n_bits = n_dp.bit_length() - 1
    core = lax.rem(d, 2)
    sibling = d + 1 - 2 * core
    other = 1 - r
    has_right = c < n_col - 1
    has_left = c > 0
    right = jnp.minimum(c + 1, n_col - 1)
    left = jnp.maximum(c - 1, 0)
    tokens, width = x_ref.shape
    full = width * n_col * 2
    half = full // 2
    heads_w = qw = ctx.shape[1]
    pairs = heads_w // 128
    n_blocks = tokens // BLOCK
    scale = HEAD_DIM**-0.5

    def to(dd, rr, cc):
        return dict(device_id=(dd, rr, cc), device_id_type=MESH)

    def bit(b):
        return lax.rem(lax.div(d, 1 << b), 2)

    def peer(b):
        return d + (1 - 2 * bit(b)) * (1 << b)

    def remote(src, dst, send, recv, dev):
        return pltpu.make_async_remote_copy(
            src_ref=src, dst_ref=dst, send_sem=send, recv_sem=recv, **dev
        )

    def at(start, size):
        return pl.ds(pl.multiple_of(start, math.gcd(size, 256)), size)

    across = to(d, other, c)

    barrier = pltpu.get_barrier_semaphore()
    pl.semaphore_signal(barrier, inc=1, **across)
    for s in range(1, n_col):
        pl.semaphore_signal(barrier, inc=1, **to(d, r, lax.rem(c + s, n_col)))
    for b in range(n_bits):
        pl.semaphore_signal(barrier, inc=1, **to(peer(b), r, c))
    pl.semaphore_wait(barrier, 1 + (n_col - 1) + n_bits)

    def block(ref, rr, j):
        return ref.at[:, at((rr * n_col + j) * width, width)]

    def hop(whole, own, rr, j, send, recv, lane, step):
        dst = block(whole, rr, j)
        return remote(
            dst if own is None else own,
            dst,
            send.at[lane, step, j],
            recv.at[lane, j],
            to(d, r, right if step == 0 else left),
        )

    def over(whole, own, j, send, recv):
        dst = block(whole, r, j)
        return remote(dst if own is None else own, dst, send, recv, across)

    def landed(dst, recv):
        return remote(dst, dst, recv, recv, across)

    def start_hop(cond, whole, own, rr, j, send, recv, lane, step):
        @pl.when(cond)
        def _():
            hop(whole, own, rr, j, send, recv, lane, step).start()

    def start_both(whole, own, rr, send, recv, lane):
        start_hop(has_right, whole, own, rr, c, send, recv, lane, 0)
        start_hop(has_left, whole, own, rr, c, send, recv, lane, 1)

    def advance(whole, rr, send, recv, lane, s, then=None):
        @pl.when(c >= s)
        def _():
            j = c - s
            landed(block(whole, rr, j), recv.at[lane, j]).wait_recv()
            start_hop(has_right, whole, None, rr, j, send, recv, lane, 0)
            if then is not None:
                then(j)

        @pl.when(c + s < n_col)
        def _():
            j = c + s
            landed(block(whole, rr, j), recv.at[lane, j]).wait_recv()
            start_hop(has_left, whole, None, rr, j, send, recv, lane, 1)
            if then is not None:
                then(j)

    def drain(whole, rr, send, recv, lane):
        for s in range(n_col):

            @pl.when((c >= s) & has_right)
            def _():
                hop(whole, None, rr, jnp.maximum(c - s, 0), send, recv, lane, 0).wait_send()

            @pl.when((c + s < n_col) & has_left)
            def _():
                j = jnp.minimum(c + s, n_col - 1)
                hop(whole, None, rr, j, send, recv, lane, 1).wait_send()

    def piece(i, k, rr):
        if i < 3:
            depth = wq_ref.shape[1] // 4
            return (
                wq_ref.at[i, at(k * depth, depth), at((1 - rr) * qw, qw)],
                wqf.at[at((rr * 4 + k) * depth, depth), i * qw : (i + 1) * qw],
            )
        if i == 3:
            depth, part = w1_ref.shape[0] // 4, w1_ref.shape[1] // 2
            return (
                w1_ref.at[at(k * depth, depth), at((1 - rr) * part, part)],
                w1f.at[at((rr * 4 + k) * depth, depth), :],
            )
        src, dst = (w2_ref, w2f) if i == 4 else (wd_ref, wdf)
        depth, part = src.shape[0] // 8, src.shape[1]
        return (
            src.at[at(((1 - rr) * 4 + k) * depth, depth), :],
            dst.at[at(k * depth, depth), at(rr * part, part)],
        )

    w_send, w_recv, y_send, y_recv = (ns[n] for n in ("w_send", "w_recv", "y_send", "y_recv"))
    s_send, s_recv = ns["s_send"], ns["s_recv"]
    upper = bit(1)
    quarter = (core + 2 * upper, core + 2 * (1 - upper))
    quarter_sib = (1 - core + 2 * upper, 1 - core + 2 * (1 - upper))

    def weight_across(i):
        src, dst = piece(i, quarter[0], r)
        return remote(src, dst, w_send.at[i], w_recv.at[i], across)

    def weight_up(i):
        dst = piece(i, quarter[0], other)[1]
        return remote(dst, dst, y_send.at[i], y_recv.at[i], to(peer(1), r, c))

    def weight_share(i, h):
        dst = piece(i, quarter[h], other)[1]
        return remote(dst, dst, s_send.at[i, h], s_recv.at[i, h], to(sibling, r, c))

    def weights_first(group):
        for i in group:
            landed(piece(i, quarter[0], other)[1], w_recv.at[i]).wait_recv()
            weight_up(i).start()
            weight_share(i, 0).start()

    def weights_second(group):
        for i in group:
            landed(piece(i, quarter[1], other)[1], y_recv.at[i]).wait_recv()
            weight_share(i, 1).start()

    def weights_wait(group):
        for i in group:
            for h in range(2):
                landed(piece(i, quarter_sib[h], other)[1], s_recv.at[i, h]).wait_recv()

    x_send, x_recv, g_send, g_recv = (ns[n] for n in ("x_send", "x_recv", "g_send", "g_recv"))
    c_send, c_recv, cx_send, cx_recv = (ns[n] for n in ("c_send", "c_recv", "cx_send", "cx_recv"))
    gb_over = over(gf, gb_ref, c, g_send.at[1, 2, c], g_recv.at[1, c])
    x_over = over(xf, x_ref, c, x_send.at[1, 2, c], x_recv.at[1, c])
    gb_over.start()
    x_over.start()
    start_both(gf, gb_ref, r, g_send, g_recv, 0)
    start_both(xf, x_ref, r, x_send, x_recv, 0)

    own = [(x_ref, block(xf, r, c)), (gb_ref, block(gf, r, c)), (cot_ref, block(cf, r, c))]
    depth = wq_ref.shape[1]
    for s in range(3):
        own.append((wq_ref.at[s, :, at(r * qw, qw)], wqf.at[at(r * depth, depth), s * qw : (s + 1) * qw]))
    depth, part = w1_ref.shape[0], w1_ref.shape[1] // 2
    own.append((w1_ref.at[:, at(r * part, part)], w1f.at[at(r * depth, depth), :]))
    for src, dst in ((w2_ref, w2f), (wd_ref, wdf)):
        depth, part = src.shape[0] // 2, src.shape[1]
        own.append((src.at[at(r * depth, depth), :], dst.at[:, at(r * part, part)]))
    own = [pltpu.make_async_copy(a, b, load_sem.at[i]) for i, (a, b) in enumerate(own)]
    for copy in own:
        copy.start()

    def tables(i, _):
        rows = at(i * BLOCK, BLOCK)
        angle = ns["places"][rows, 1:2].astype(F32) * ns["freq"][...]
        cos_ref[rows, :] = jnp.cos(angle)
        sin_ref[rows, :] = jnp.sin(angle)
        return 0

    landed(block(gf, other, c), g_recv.at[1, c]).wait_recv()
    start_both(gf, None, other, g_send, g_recv, 1)
    landed(block(xf, other, c), x_recv.at[1, c]).wait_recv()
    start_both(xf, None, other, x_send, x_recv, 1)
    for i in range(4):
        weight_across(i).start()

    def cot_over(j):
        return over(cf, None, j, cx_send.at[j], cx_recv.at[j])

    over(cf, cot_ref, c, cx_send.at[c], cx_recv.at[c]).start()
    for i in range(4, 6):
        weight_across(i).start()

    def start_cot(s):
        start_hop(has_right & (c == s), cf, cot_ref, r, c, c_send, c_recv, 0, 0)
        start_hop(has_left & (c == n_col - 1 - s), cf, cot_ref, r, c, c_send, c_recv, 0, 1)

    start_cot(0)
    lax.fori_loop(0, n_blocks, tables, 0)
    for s in range(1, n_col):
        for lane in range(2):
            rr = r if lane == 0 else other
            advance(gf, rr, g_send, g_recv, lane, s)
            advance(xf, rr, x_send, x_recv, lane, s)
        start_cot(s)
        if s == 1:
            weights_first(range(4))
        if s == 2:
            weights_second(range(4))
            weights_first(range(4, 6))

    def advance_cot(s):
        advance(cf, r, c_send, c_recv, 0, s, then=lambda j: cot_over(j).start())

    weights_second(range(4, 6))
    for copy in own:
        copy.wait()

    gain = gf[0:1, :]
    shift = gf[8:9, :]

    def norm_rows(i, _):
        rows = at(i * 64, 64)
        v = xf[rows, :].astype(F32)
        mu = jnp.sum(v, axis=1, keepdims=True) * (1.0 / full)
        v = v - mu
        inv = lax.rsqrt(jnp.sum(v * v, axis=1, keepdims=True) * (1.0 / full) + NORM_EPSILON)
        ns["mean"][rows, :] = mu
        ns["rstd"][rows, :] = inv
        normed[rows, :] = (v * inv * gain + shift).astype(BF)
        return 0

    lax.fori_loop(0, tokens // 64, norm_rows, 0)
    advance_cot(1)
    weights_wait(range(4))

    lane_at = lax.broadcasted_iota(jnp.int32, (1, 128), 1)
    first = lane_at % HEAD_DIM < ROT_DIM // 2
    low_head = lane_at < HEAD_DIM

    def turn(v, cos, sin, sign):
        up = pltpu.roll(v, 128 - ROT_DIM // 2, 1)
        down = pltpu.roll(v, ROT_DIM // 2, 1)
        swapped = jnp.where(first, -up, down) * sin
        return v * cos + swapped if sign > 0 else v * cos - swapped

    def qkv_rows(i, _):
        rows = at(i * BLOCK, BLOCK)
        mixed = dot(normed[rows, :], wqf[...], NN)
        cos, sin = cos_ref[rows, :], sin_ref[rows, :]
        for s, dst in enumerate((q_s, k_s, v_s)):
            for t in range(pairs):
                lanes = slice(s * qw + t * 128, s * qw + (t + 1) * 128)
                v = mixed[:, lanes] + ns["qkv_bias"][s : s + 1, t * 128 : (t + 1) * 128]
                dst[t, rows, :] = (turn(v, cos, sin, 1) if s < 2 else v).astype(BF)
        return 0

    lax.fori_loop(0, n_blocks, qkv_rows, 0)
    advance_cot(2)

    def fc1_rows(i, _):
        rows = at(i * BLOCK, BLOCK)
        for h in range(2):
            cols = slice(h * 512, (h + 1) * 512)
            v = dot(normed[rows, :], w1f[:, cols], NN) + ns["fc1_bias"][:, cols]
            th = jnp.tanh(GELU_A * (v + GELU_B * v * v * v))
            hidden[rows, cols] = (0.5 * v * (1.0 + th)).astype(BF)
            slope = 0.5 * (1.0 + th) + 0.5 * v * (1.0 - th * th) * (
                GELU_A * (1.0 + 3.0 * GELU_B * v * v)
            )
            pg[rows, cols] = slope.astype(BF)
        return 0

    lax.fori_loop(0, n_blocks, fc1_rows, 0)

    def set_bias(i):
        keys = (i + 1) * BLOCK
        rows = slice(i * BLOCK, keys)
        row_at = lax.broadcasted_iota(jnp.int32, (BLOCK, keys), 0) + i * BLOCK
        key_at = lax.broadcasted_iota(jnp.int32, (BLOCK, keys), 1)
        allowed = (ns["places"][rows, 0:1] == ns["seg_row"][:, :keys]) & (row_at >= key_at)
        bias_s[:, :keys] = jnp.where(allowed, 0.0, MASKED_SCORE)

    def mine(h, v):
        return jnp.where(low_head if h == 0 else ~low_head, v, jnp.zeros_like(v))

    def forward_block(i):
        keys = (i + 1) * BLOCK
        rows = slice(i * BLOCK, keys)
        set_bias(i)

        def pair(t, _):
            q, k, v = q_s[t, rows, :], k_s[t, :keys, :], v_s[t, :keys, :]
            outs = []
            logs = lse[rows, :]
            for h in range(2):
                s = dot(mine(h, q), k, NT) * scale + bias_s[:, :keys]
                top = jnp.max(s, axis=1, keepdims=True)
                e = jnp.exp(s - top)
                total = jnp.sum(e, axis=1, keepdims=True)
                low = (e * (1.0 / total)).astype(BF)
                outs.append(dot(low, v, NN))
                logs = jnp.where(lane_at == 2 * t + h, top + jnp.log(total), logs)
            lse[rows, :] = logs
            ctx[rows, at(t * 128, 128)] = jnp.where(low_head, outs[0], outs[1]).astype(BF)
            return 0

        lax.fori_loop(0, pairs, pair, 0)

    lse[...] = jnp.zeros_like(lse)
    for i in range(n_blocks):
        if i == n_blocks - 1:
            advance_cot(3)
        forward_block(i)
    weights_wait(range(4, 6))

    rs_send, rs_recv, xs_send, xs_recv = (ns[n] for n in ("rs_send", "rs_recv", "xs_send", "xs_recv"))
    ag_send, ag_recv, part_sem = (ns[n] for n in ("ag_send", "ag_recv", "part_sem"))
    g1, g2, gd, gq = ns["g1"], ns["g2"], ns["gd"], ns["gq"]
    tensors = dict(
        fc1=(0, g1, ns["rb1"], ns["stage1"], half),
        fc2=(1, g2, ns["rb2"], ns["stage1"], hidden.shape[1]),
        dense=(2, gd, ns["rbd"], ns["staged"], heads_w),
        qkv=(3, gq, ns["rbq"], ns["stageq"], half),
    )
    results = dict(fc1=ns["f1"], fc2=ns["f2"], dense=ns["fd"], qkv=ns["fq"])
    mine_at, theirs_at = r * half, other * half
    starts = (mine_at, theirs_at)

    def slab(ref, p, rows):
        return ref.at[p, :, rows, :] if len(ref.shape) == 4 else ref.at[p, rows, :]

    def offset(rows, upto):
        off = 0
        for b in range(upto):
            off = off + bit(b) * (rows >> (b + 1))
        return off

    def landing(rows, b):
        return slice(rows - (rows >> b), rows - (rows >> (b + 1)))

    def sum_copy(name, p, b):
        n, g, rb, _, rows = tensors[name]
        size = rows >> (b + 1)
        return remote(
            slab(g, p, at(offset(rows, b) + (1 - bit(b)) * size, size)),
            slab(rb, p, landing(rows, b)),
            rs_send.at[n, p, b],
            rs_recv.at[n, p, b],
            to(peer(b), r, c),
        )

    def place(name, rr, off, size):
        if name == "fc1":
            return ns["f1"].at[at(off, size), at(rr * hidden.shape[1], hidden.shape[1])]
        if name == "qkv":
            return ns["fq"].at[:, at(off, size), at(rr * qw, qw)]
        return results[name].at[rr, at(off, size), :]

    def kept(name, p):
        _, g, _, _, rows = tensors[name]
        size = rows >> n_bits
        off = offset(rows, n_bits)
        return slab(g, p, at(off, size)), off, size

    def part_copy(name):
        src, off, size = kept(name, 0)
        return pltpu.make_async_copy(src, place(name, r, off, size), part_sem.at[tensors[name][0]])

    def swap_copy(name):
        src, off, size = kept(name, 1)
        n = tensors[name][0]
        return remote(src, place(name, r, off, size), xs_send.at[n], xs_recv.at[n], across)

    def sum_next(name, p, b):
        n, g, rb, stage, rows = tensors[name]
        size = rows >> (b + 1)
        off = offset(rows, b + 1)
        sum_copy(name, p, b).wait_recv()
        four = len(g.shape) == 4
        chunk = min(size, 128)
        dst = stage.at[:, :size, :] if four else stage.at[:size, :]
        copy = pltpu.make_async_copy(slab(rb, p, landing(rows, b)), dst, stage_sem.at[0])
        copy.start()
        copy.wait()

        def add(i, _):
            if four:
                there = (p, slice(None), at(off + i * chunk, chunk), slice(None))
                here = (slice(None), at(i * chunk, chunk), slice(None))
            else:
                there = (p, at(off + i * chunk, chunk), slice(None))
                here = (at(i * chunk, chunk), slice(None))
            g[there] = (g[there].astype(F32) + stage[here].astype(F32)).astype(BF)
            return 0

        lax.fori_loop(0, size // chunk, add, 0)
        if b + 1 < n_bits:
            sum_copy(name, p, b + 1).start()
        elif p == 0:
            part_copy(name).start()
        else:
            swap_copy(name).start()

    def sum_rest(name):
        for p in (1, 0):
            for b in range(1, n_bits):
                sum_next(name, p, b)

    def rows_of(name, off, size):
        ref = results[name]
        return ref.at[at(off, size), :] if name == "fc1" else ref.at[:, at(off, size), :]

    def spread_copy(name, b):
        n, rows = tensors[name][0], tensors[name][4]
        ref = rows_of(name, offset(rows, b + 1), rows >> (b + 1))
        return remote(ref, ref, ag_send.at[n, b], ag_recv.at[n, b], to(peer(b), r, c))

    def spread_landed(name, b):
        n, rows = tensors[name][0], tensors[name][4]
        size = rows >> (b + 1)
        return landed(rows_of(name, offset(rows, b) + (1 - bit(b)) * size, size), ag_recv.at[n, b])

    def spread_first(name):
        _, off, size = kept(name, 0)
        part_copy(name).wait()
        landed(place(name, other, off, size), xs_recv.at[tensors[name][0]]).wait_recv()
        spread_copy(name, n_bits - 1).start()

    def spread_next(name, b):
        spread_landed(name, b).wait_recv()
        if b > 0:
            spread_copy(name, b - 1).start()

    def spread_rest(name):
        for b in reversed(range(1, n_bits)):
            spread_next(name, b)

    def finish(name):
        for b in range(n_bits):
            for p in range(2):
                sum_copy(name, p, b).wait_send()
            spread_copy(name, b).wait_send()
        swap_copy(name).wait_send()

    def fc2_grad(p):
        def body(i, _):
            cols = at(i * BLOCK, BLOCK)
            g2[p, cols, :] = dot(hidden[:, cols], cf[:, at(starts[p], half)], TN).astype(BF)
            return 0

        lax.fori_loop(0, hidden.shape[1] // BLOCK, body, 0)
        sum_copy("fc2", p, 0).start()

    def fc1_grad(p):
        def body(i, _):
            g1[p, at(i * BLOCK, BLOCK), :] = dot(
                normed[:, at(starts[p] + i * BLOCK, BLOCK)], pg[...], TN
            ).astype(BF)
            return 0

        lax.fori_loop(0, half // BLOCK, body, 0)
        sum_copy("fc1", p, 0).start()

    def dense_grad(p):
        gd[p] = dot(ctx[...], cf[:, at(starts[p], half)], TN).astype(BF)
        sum_copy("dense", p, 0).start()

    def qkv_grad(p):
        def body(i, _):
            v = dot(normed[:, at(starts[p] + i * BLOCK, BLOCK)], mg[...], TN).astype(BF)
            for s in range(3):
                gq[p, s, at(i * BLOCK, BLOCK), :] = v[:, s * qw : (s + 1) * qw]
            return 0

        lax.fori_loop(0, half // BLOCK, body, 0)
        sum_copy("qkv", p, 0).start()

    ox_send, ox_recv, oz_send, oz_recv = (ns[n] for n in ("ox_send", "ox_recv", "oz_send", "oz_recv"))
    free_sem = ns["free_sem"]
    outputs = ((xf, ns["rzo"], dk_s), (cf, ns["rzn"], dv_s))

    def out_part(n, rows, start):
        if n == 0:
            return dot(ctx[rows, :], wdf[:, at(start, half)], NN) + dot(
                hidden[rows, :], w2f[:, at(start, half)], NN
            )
        return dot(mg[rows, :], wqf[at(start, half), :], NT) + dot(
            pg[rows, :], w1f[at(start, half), :], NT
        )

    def part_over(n, i):
        buf = outputs[n][0]
        rows = slice(i * BLOCK, (i + 1) * BLOCK)
        return remote(
            buf.at[rows, :half], buf.at[rows, half:], ox_send.at[n, i], ox_recv.at[n, i], across
        )

    def send_theirs(n, i):
        rows = slice(i * BLOCK, (i + 1) * BLOCK)
        outputs[n][0][rows, :half] = out_part(n, rows, theirs_at).astype(BF)
        part_over(n, i).start()

    def part_on(n, i, s):
        buf, landing_z, _ = outputs[n]
        rows = slice(i * BLOCK, (i + 1) * BLOCK)
        j = lax.rem(c + s, n_col)
        return remote(
            buf.at[rows, at(j * width, width)],
            landing_z.at[s - 1, rows, :],
            oz_send.at[n, i, s - 1],
            oz_recv.at[n, i, s - 1],
            to(d, r, j),
        )

    def scatter(n, i):
        buf, _, keep = outputs[n]
        rows = slice(i * BLOCK, (i + 1) * BLOCK)
        part_over(n, i).wait()
        v = out_part(n, rows, mine_at) + buf[rows, half:].astype(F32)
        bias_s[:, :half] = v
        buf[rows, :half] = v.astype(BF)
        for t in range(width // 128):
            keep[t, rows, :] = bias_s[:, at(c * width + t * 128, 128)]
        for s in range(1, n_col):
            part_on(n, i, s).start()

    stagez = ns["stagez"]

    def collect(n):
        _, landing_z, keep = outputs[n]
        for s in range(1, n_col):
            for i in range(n_blocks):
                part_on(n, i, s).wait_recv()
            load = pltpu.make_async_copy(landing_z.at[s - 1], stagez.at[0], stage_sem.at[1])
            load.start()
            load.wait()

            def add(i, _):
                rows = at(i * BLOCK, BLOCK)
                for t in range(width // 128):
                    keep[t, rows, :] += stagez[0, rows, t * 128 : (t + 1) * 128].astype(F32)
                return 0

            lax.fori_loop(0, n_blocks, add, 0)

    def backward_block(i):
        keys = (i + 1) * BLOCK
        rows = slice(i * BLOCK, keys)
        set_bias(i)

        def pair(t, _):
            lanes = at(t * 128, 128)
            q, k, v = q_s[t, rows, :], k_s[t, :keys, :], v_s[t, :keys, :]
            grad = dctx[rows, lanes]
            query_grads = []
            for h in range(2):
                qh, gh = mine(h, q), mine(h, grad)
                log_total = jnp.sum(
                    jnp.where(lane_at == 2 * t + h, lse[rows, :], 0.0), axis=1, keepdims=True
                )
                p = jnp.exp(dot(qh, k, NT) * scale + bias_s[:, :keys] - log_total)
                dp = dot(gh, v, NT)
                dv_s[t, :keys, :] += dot(p.astype(BF), gh, TN)
                centre = jnp.sum(p * dp, axis=1, keepdims=True)
                ds = (p * (dp - centre) * scale).astype(BF)
                query_grads.append(dot(ds, k, NN))
                dk_s[t, :keys, :] += dot(ds, qh, TN)
            dq = jnp.where(low_head, query_grads[0], query_grads[1])
            mg[rows, lanes] = turn(dq, cos_ref[rows, :], sin_ref[rows, :], -1).astype(BF)
            return 0

        lax.fori_loop(0, pairs, pair, 0)

    def grad_rows(i, _):
        rows = at(i * BLOCK, BLOCK)
        dctx[rows, :] = dot(cf[rows, :], wdf[...], NT).astype(BF)
        for h in range(2):
            cols = slice(h * 512, (h + 1) * 512)
            v = dot(cf[rows, :], w2f[cols, :], NT)
            pg[rows, cols] = (v * pg[rows, cols].astype(F32)).astype(BF)
        return 0

    fc2_grad(0)
    for lane in range(2):
        rr = r if lane == 0 else other
        drain(gf, rr, g_send, g_recv, lane)
        drain(xf, rr, x_send, x_recv, lane)
    gb_over.wait_send()
    x_over.wait_send()
    pl.semaphore_signal(free_sem.at[0], inc=1, **across)
    pl.semaphore_wait(free_sem.at[0], 1)
    for i in range(n_blocks):
        send_theirs(0, i)
    for s in range(n_col):
        landed(block(cf, other, s), cx_recv.at[s]).wait_recv()
    fc2_grad(1)
    sum_next("fc2", 0, 0)
    lax.fori_loop(0, n_blocks, grad_rows, 0)
    sum_next("fc2", 1, 0)
    fc1_grad(1)
    fc1_grad(0)
    sum_next("fc1", 1, 0)
    dk_s[...] = jnp.zeros_like(dk_s)
    dv_s[...] = jnp.zeros_like(dv_s)
    for i in range(n_blocks):
        backward_block(i)
        if i == 1:
            sum_next("fc1", 0, 0)
    for t in range(pairs):
        lanes = slice(qw + t * 128, qw + (t + 1) * 128)
        mg[:, lanes] = turn(dk_s[t], cos_ref[...], sin_ref[...], -1).astype(BF)
        lanes = slice(2 * qw + t * 128, 2 * qw + (t + 1) * 128)
        mg[:, lanes] = dv_s[t].astype(BF)
    for p in (1, 0):
        dense_grad(p)
    for p in (1, 0):
        qkv_grad(p)
    sum_rest("fc2")
    drain(cf, r, c_send, c_recv, 0)
    for s in range(n_col):
        cot_over(s).wait_send()
    pl.semaphore_signal(free_sem.at[1], inc=1, **across)
    for name in ("dense", "qkv"):
        for p in (1, 0):
            sum_next(name, p, 0)
    pl.semaphore_wait(free_sem.at[1], 1)
    for i in range(2):
        send_theirs(1, i)
    for i in range(n_blocks):
        scatter(0, i)
    sum_rest("fc1")
    for i in range(2, n_blocks):
        send_theirs(1, i)
    spread_first("fc2")
    for i in range(2):
        scatter(1, i)
    sum_rest("dense")
    sum_rest("qkv")
    spread_first("fc1")

    stage_x = stagez.at[1]
    load = pltpu.make_async_copy(x_ref, stage_x, stage_sem.at[2])
    load.start()
    collect(0)
    load.wait()

    def out_final(i, _):
        rows = at(i * BLOCK, BLOCK)
        for t in range(width // 128):
            lanes = slice(t * 128, (t + 1) * 128)
            v = stagez[1, rows, lanes].astype(F32) + dk_s[t, rows, :] + ns["out_bias"][:, lanes]
            ns["y_out"][rows, lanes] = v.astype(BF)
        return 0

    lax.fori_loop(0, n_blocks, out_final, 0)
    for i in range(2, n_blocks):
        scatter(1, i)
    spread_rest("fc2")
    spread_first("dense")
    spread_first("qkv")

    collect(1)
    tot, small_v, small_r = ns["tot"], ns["small_v"], ns["small_r"]
    grads = ns["small"]
    small_v[...] = jnp.zeros_like(small_v)
    n_mixed, n_pre = mg.shape[1], pg.shape[1]
    base = n_mixed + n_pre

    def norm_sums(i, _):
        rows = at(i * BLOCK, BLOCK)
        mu, inv = ns["mean"][rows, :], ns["rstd"][rows, :]
        one = jnp.zeros((BLOCK, 1), F32)
        two = jnp.zeros((BLOCK, 1), F32)
        for t in range(width // 128):
            lanes = slice(t * 128, (t + 1) * 128)
            g = dv_s[t, rows, :]
            hat = (stagez[1, rows, lanes].astype(F32) - mu) * inv
            sg = g * ns["gain_own"][:, lanes]
            one = one + jnp.sum(sg, axis=1, keepdims=True)
            two = two + jnp.sum(sg * hat, axis=1, keepdims=True)
            lo = base + width + t * 128
            small_v[0:1, lo : lo + 128] += jnp.sum(g * hat, axis=0, keepdims=True)
            lo = base + 2 * width + t * 128
            small_v[0:1, lo : lo + 128] += jnp.sum(g, axis=0, keepdims=True)
        packed = jnp.where(lane_at == 0, one, jnp.where(lane_at == 1, two, 0.0))
        tot[0, :, rows] = jnp.transpose(packed)[0:8, :]
        small_v[0:1, :n_mixed] += jnp.sum(mg[rows, :].astype(F32), axis=0, keepdims=True)
        small_v[0:1, n_mixed:base] += jnp.sum(pg[rows, :].astype(F32), axis=0, keepdims=True)
        return 0

    lax.fori_loop(0, n_blocks, norm_sums, 0)
    tot_send, tot_recv = ns["tot_send"], ns["tot_recv"]
    swap = remote(tot.at[0], tot.at[1], tot_send.at[0], tot_recv.at[0], across)
    swap.start()
    load = pltpu.make_async_copy(cot_ref, stagez.at[0], stage_sem.at[1])
    load.start()
    load.wait()

    def cot_sums(i, _):
        rows = at(i * BLOCK, BLOCK)
        small_v[0:1, base : base + width] += jnp.sum(
            stagez[0, rows, :].astype(F32), axis=0, keepdims=True
        )
        return 0

    lax.fori_loop(0, n_blocks, cot_sums, 0)
    sm_send, sm_recv = ns["sm_send"], ns["sm_recv"]

    def small_copy(b):
        return remote(small_v, small_r.at[b], sm_send.at[b], sm_recv.at[b], to(peer(b), r, c))

    small_copy(0).start()
    swap.wait()
    tot[0] = tot[0] + tot[1]
    tot_copies = [
        remote(
            tot.at[0], tot.at[1 + s], tot_send.at[s], tot_recv.at[s], to(d, r, lax.rem(c + s, n_col))
        )
        for s in range(1, n_col)
    ]
    for copy in tot_copies:
        copy.start()
    for b in range(n_bits):
        small_copy(b).wait()
        small_v[...] = small_v[...] + small_r[b]
        if b + 1 < n_bits:
            small_copy(b + 1).start()
    grads[...] = small_v[...]
    for copy in tot_copies:
        copy.wait()
    tot[1] = tot[0]
    for s in range(1, n_col):
        tot[1] = tot[1] + tot[1 + s]

    def in_final(i, _):
        rows = at(i * BLOCK, BLOCK)
        mu, inv = ns["mean"][rows, :], ns["rstd"][rows, :]
        sums = jnp.transpose(
            jnp.concatenate([tot[1, :, rows], jnp.zeros((120, BLOCK), F32)], axis=0)
        ) * (1.0 / full)
        one, two = sums[:, 0:1], sums[:, 1:2]
        for t in range(width // 128):
            lanes = slice(t * 128, (t + 1) * 128)
            hat = (stagez[1, rows, lanes].astype(F32) - mu) * inv
            sg = dv_s[t, rows, :] * ns["gain_own"][:, lanes]
            ns["in_grad"][rows, lanes] = stagez[0, rows, lanes].astype(F32) + inv * (
                sg - one - hat * two
            )
        return 0

    lax.fori_loop(0, n_blocks, in_final, 0)

    for name in ("fc1", "dense", "qkv"):
        spread_rest(name)
    for name in tensors:
        spread_next(name, 0)
    for name in tensors:
        finish(name)
    for i in range(6):
        weight_across(i).wait_send()
        weight_up(i).wait_send()
        for h in range(2):
            weight_share(i, h).wait_send()
    for n in range(2):
        for i in range(n_blocks):
            for s in range(1, n_col):
                part_on(n, i, s).wait_send()


def local(
    block_input,
    segment_ids,
    positions,
    ln_gain,
    ln_bias,
    qkv_weight,
    qkv_bias,
    dense_weight,
    dense_bias,
    fc1_weight,
    fc1_bias,
    fc2_weight,
    fc2_bias,
    cotangent,
):
    n_col = lax.axis_size("col")
    n_dp = lax.axis_size("dp")
    n_bits = n_dp.bit_length() - 1
    tokens, width = block_input.shape
    full = width * n_col * 2
    half = full // 2
    qw = qkv_weight.shape[2] // 2
    hid = fc1_weight.shape[1] // 2
    pairs = qw // 128
    small_w = 3 * qw + hid + 3 * width
    gb = jnp.concatenate(
        [
            jnp.broadcast_to(ln_gain.astype(F32)[None], (8, width)),
            jnp.broadcast_to(ln_bias.astype(F32)[None], (8, width)),
        ],
        axis=0,
    )
    lane = np.arange(128) % HEAD_DIM
    steps = (lane % (ROT_DIM // 2)).astype(np.float32)
    freq = np.exp(steps * np.float32(-2.0 * math.log(10000.0) / ROT_DIM), dtype=np.float32)
    freq = jnp.asarray(np.where(lane < ROT_DIM, freq, np.float32(0.0))[None])
    hbm = pl.BlockSpec(memory_space=pl.ANY)
    vmem = pl.BlockSpec(memory_space=pltpu.VMEM)
    dma = pltpu.SemaphoreType.DMA
    bits = max(n_bits, 1)
    sds = jax.ShapeDtypeStruct
    outs = (
        (vmem, sds((tokens, width), BF)),
        (vmem, sds((tokens, width), F32)),
        (vmem, sds((8, small_w), F32)),
        (hbm, sds((half, 2 * hid), BF)),
        (hbm, sds((2, hid, half), BF)),
        (hbm, sds((2, qw, half), BF)),
        (hbm, sds((3, half, 2 * qw), BF)),
        (hbm, sds((2, half, hid), BF)),
        (hbm, sds((2, hid, half), BF)),
        (hbm, sds((2, qw, half), BF)),
        (hbm, sds((2, 3, half, qw), BF)),
        (hbm, sds((n_col - 1, tokens, width), BF)),
        (hbm, sds((n_col - 1, tokens, width), BF)),
    )
    v = pltpu.VMEM
    scratch = [
        v((tokens, full), BF),
        v((tokens, full), BF),
        v((16, full), F32),
        v((full, 3 * qw), BF),
        v((full, hid), BF),
        v((hid, full), BF),
        v((qw, full), BF),
        v((tokens, full), BF),
        v((tokens, hid), BF),
        v((tokens, hid), BF),
        v((pairs, tokens, 128), BF),
        v((pairs, tokens, 128), BF),
        v((pairs, tokens, 128), BF),
        v((pairs, tokens, 128), F32),
        v((pairs, tokens, 128), F32),
        v((BLOCK, tokens), F32),
        v((tokens, 128), F32),
        v((tokens, 128), F32),
        v((tokens, qw), BF),
        v((tokens, qw), BF),
        v((tokens, 3 * qw), BF),
        v((tokens, 128), F32),
        v((2, half, hid), BF),
        v((2, hid, half), BF),
        v((2, qw, half), BF),
        v((2, 3, half, qw), BF),
        v((half // 2, hid), BF),
        v((qw // 2, half), BF),
        v((3, half // 2, qw), BF),
        v((2, tokens, width), BF),
        v((tokens, 1), F32),
        v((tokens, 1), F32),
        v((n_col + 1, 8, tokens), F32),
        v((8, small_w), F32),
        v((bits, 8, small_w), F32),
        dma((2, 3, n_col)),
        dma((2, n_col)),
        dma((2, 3, n_col)),
        dma((2, n_col)),
        dma((1, 2, n_col)),
        dma((1, n_col)),
        dma((n_col,)),
        dma((n_col,)),
        dma((6,)),
        dma((6,)),
        dma((6,)),
        dma((6,)),
        dma((6, 2)),
        dma((6, 2)),
        dma((9,)),
        dma((4, 2, bits)),
        dma((4, 2, bits)),
        dma((4,)),
        dma((4,)),
        dma((4, bits)),
        dma((4, bits)),
        dma((4,)),
        dma((3,)),
        dma((2, tokens // BLOCK)),
        dma((2, tokens // BLOCK)),
        dma((2, tokens // BLOCK, n_col - 1)),
        dma((2, tokens // BLOCK, n_col - 1)),
        dma((n_col,)),
        dma((n_col,)),
        dma((bits,)),
        dma((bits,)),
        pltpu.SemaphoreType.REGULAR((2,)),
    ]
    res = pl.pallas_call(
        functools.partial(kernel, n_dp, n_col),
        out_shape=tuple(o[1] for o in outs),
        in_specs=[hbm] * 6 + [vmem] * 8,
        out_specs=tuple(o[0] for o in outs),
        scratch_shapes=scratch,
        compiler_params=pltpu.CompilerParams(
            collective_id=0,
            has_side_effects=True,
            vmem_limit_bytes=64 * 2**20,
            fuse_transposed_lhs_in_matmul=True,
        ),
        cost_estimate=pl.CostEstimate(
            flops=45 * 10**9, bytes_accessed=64 * 2**20, transcendentals=8 * 2**20
        ),
    )(
        block_input,
        cotangent,
        jnp.transpose(qkv_weight, (1, 0, 2)),
        fc1_weight,
        fc2_weight,
        dense_weight,
        gb,
        jnp.stack([segment_ids, positions], axis=1),
        segment_ids.reshape(1, tokens),
        freq,
        qkv_bias.reshape(3, qw),
        fc1_bias.reshape(1, hid),
        (dense_bias + fc2_bias).reshape(1, width),
        ln_gain.astype(F32).reshape(1, width),
    )
    y_out, in_grad, small, f1, f2, fd, fq = res[:7]
    small = small[0]
    n_mixed = 3 * qw
    base = n_mixed + hid
    bias_grad, gain_grad, shift_grad = (
        small[base + i * width : base + (i + 1) * width] for i in range(3)
    )
    return (
        y_out,
        in_grad,
        gain_grad,
        shift_grad,
        jnp.transpose(fq.astype(F32), (1, 0, 2)),
        small[:n_mixed].reshape(qkv_bias.shape),
        fd.reshape(dense_weight.shape).astype(F32),
        bias_grad,
        f1.astype(F32),
        small[n_mixed:base].reshape(fc1_bias.shape),
        f2.reshape(fc2_weight.shape).astype(F32),
        bias_grad,
    )


def solution(mesh):
    return jax.shard_map(
        local,
        mesh=mesh,
        in_specs=(
            P("dp", ("row", "col")),
            P("dp"),
            P("dp"),
            P(("row", "col")),
            P(("row", "col")),
            P("row", None, "col"),
            P(None, "col", "row", None),
            P("col", "row"),
            P(("row", "col")),
            P("row", "col"),
            P("col", "row", None),
            P("col", "row"),
            P(("row", "col")),
            P("dp", ("row", "col")),
        ),
        out_specs=(
            P("dp", ("row", "col")),
            P("dp", ("row", "col")),
            P(("row", "col")),
            P(("row", "col")),
            P("row", None, "col"),
            P(None, "col", "row", None),
            P("col", "row"),
            P(("row", "col")),
            P("row", "col"),
            P("col", "row", None),
            P("col", "row"),
            P(("row", "col")),
        ),
        check_vma=False,
    )
```

time: 1300 us -> 329 us (0.25)
  waiting for transfers between devices: 935 us -> 0 us
  Pallas kernels: 0 us -> 291 us
  matrix products: 125 us -> 0 us
  local copies, waits for them, and re-layouts: 84.2 us -> 9.93 us
  blocking collectives: 68.2 us -> 0 us
  other arithmetic: 49.8 us -> 20.2 us
  between operations: 14.8 us -> 1.11 us
    psum x1 -> x0, waiting for transfers between devices: 427 us -> none  [local(): lax.psum((gain_grad, shift_grad, qkv_grad, qkv_bias_grad, dense_grad, bia...]
    reduce_scatter x6 -> x0, waiting for transfers between devices: 323 us -> none  [the longest x1 102 us: local(): lax.psum_scatter(part_up, 'row', scatter_dimension=1, tiled=True)]
    pallas_call x0 -> x1, Pallas kernels: none -> 291 us  [local(): pl.pallas_call(functools.partial(kernel, n_dp, n_col), out_shape=tuple((o...]
    all_gather x6 -> x0, waiting for transfers between devices: 183 us -> none  [the longest x1 51.2 us: local(): lax.all_gather(hidden, 'row', axis=1, tiled=True)]
    dot_general x26 -> x0, matrix products: 125 us -> none  [the longest x1 10.8 us: local(): jnp.einsum('tb,ab->ta', cot_rows, fc2_weight, preferred_element_type=jnp....]
    all_gather x2 -> x0, blocking collectives: 34.8 us -> none  [the longest x1 17.9 us: local(): lax.all_gather(ln_gain, ('row', 'col'), axis=0, tiled=True)]
    psum x2 -> x0, blocking collectives: 33.4 us -> none  [the longest x1 21.9 us: local(): lax.psum((jnp.sum(scaled_grad, axis=-1), jnp.sum(scaled_grad * scaled_her...]
    reduce_sum x8 -> x0, other arithmetic: 24.3 us -> none  [the longest x1 7.43 us: local(): jnp.sum(pre_grad.astype(jnp.float32), axis=0).reshape(fc1_bias.shape)]
  transfers between devices with their start and end apart: 13 -> 0, of which waited for: 11 -> 0; matrix products, arithmetic and copies ran while one was open for 17% -> 0% of each run, Pallas kernels for 0% -> 0%
where the time goes in v2:
time: 329 us; the launch traced here: 322 us
  Pallas kernels  291 us (88%)
  other arithmetic  20.2 us (6%)
  local copies, waits for them, and re-layouts  9.93 us (3%)
    pallas_call x1, Pallas kernels, local(): pl.pallas_call(functools.partial(kernel, n_dp, n_col), out_shape=tuple((o...  291 us
    convert_element_type x1, other arithmetic, local(): f2.reshape(fc2_weight.shape).astype(F32)  6.79 us

profile of v2, /device:TPU:0, one launch (start us, length us, event | category | flops | bytes accessed | tf_op | source)
XLA Modules:
  0.0 322.1 jit_solution(11172107275498117042)
XLA Ops:
  0.6 0.7 pad_add_fusion
  1.4 1.0 copy.31.refs_7_
  2.4 0.7 broadcast_in_dim.6
  3.0 0.7 broadcast_in_dim.7
  3.7 0.6 pad_maximum_fusion.refs_6_
  4.3 1.3 copy.35
  5.6 1.3 add.3
  6.8 1.2 convert_element_type.23
  8.1 290.8 %shard_map.238 = (bf16[1024,256]{1,0:T(8,128)(2,1)}, f32[1024,256]{1,0:T(8,128)}, f32[8,2560]{1,0:T(8,128)}, bf16[1024,2048]{1,0:T(8,128)(2,1)}, bf16[2,1024,102...) custom-call(bf16[1024,256]{1,0:T(8,128)(2,1)} %refs_0_.1, ...), custom_call_target="tpu_custom_call" | custom-call | flops 44999999488 | bytes 67108864 | tf_op jit(solution)/shard_map/pallas_call | solution.py:959
  298.9 1.3 fusion
  300.2 0.0 copy-start.5
  300.2 1.4 slice_bitcast_fusion
  301.5 1.3 slice.36
  302.8 0.0 copy-start
  302.8 6.8 %bitcast_convert_fusion = f32[2048,1024]{1,0:T(8,128)} fusion(bf16[2,1024,1024]{2,1,0:T(8,128)(2,1)} %get-tuple-element.25), kind=kLoop, calls=%fused_computation.1 | loop fusion | flops 2097152 | bytes 12582912 | tf_op jit(solution)/shard_map/convert_element_type | solution.py:1008
  309.6 0.0 copy-done
  309.6 0.0 copy-start.1
  309.6 4.4 %convert_element_type.27 = f32[1024,2048]{1,0:T(8,128)} convert(bf16[1024,2048]{1,0:T(8,128)(2,1)S(1)} %copy-done) | non-fusion elementwise | flops 2097152 | bytes 12582912 | tf_op jit(solution)/shard_map/convert_element_type | solution.py:1006
  314.1 0.0 copy-done.1
  314.1 0.0 copy-start.2
  314.1 0.0 copy-start.4
  314.1 3.6 %convert_bitcast_fusion = f32[1024,3,512]{2,0,1:T(8,128)} fusion(bf16[3,1024,512]{2,1,0:T(8,128)(2,1)S(1)} %copy-done.1), kind=kLoop, calls=%fused_computation | loop fusion | flops 1572864 | bytes 9437184 | tf_op jit(solution)/shard_map/transpose | solution.py:1002
  317.7 0.0 copy-start.3
  317.7 0.0 copy-done.2
  317.7 1.6 bitcast_convert_fusion.1
  319.3 0.0 copy-done.5
  319.3 0.6 copy.39
  319.9 0.0 copy-done.4
  319.9 0.8 copy.40
  320.7 0.0 copy-done.3
  320.7 1.0 copy.41
Async XLA Ops:
  300.2 19.1 %copy-start.5 = (f32[1,256]{1,0:T(1,128)}, f32[1,256]{1,0:T(1,128)S(1)}, u32[]{:S(2)}) copy-start(f32[1,256]{1,0:T(1,128)S(1)} %get-tuple-element.62) | copy-start | bytes 3076
  302.8 6.8 %copy-start = (bf16[1024,2048]{1,0:T(8,128)(2,1)S(1)}, bf16[1024,2048]{1,0:T(8,128)(2,1)}, u32[]{:S(2)}) copy-start(bf16[1024,2048]{1,0:T(8,128)(2,1)} %get-tuple-element.24) | copy-start | bytes 12582916
  309.6 4.4 %copy-start.1 = (bf16[3,1024,512]{2,1,0:T(8,128)(2,1)S(1)}, bf16[3,1024,512]{2,1,0:T(8,128)(2,1)}, u32[]{:S(2)}) copy-start(bf16[3,1024,512]{2,1,0:T(8,128)(2,1)} %get-tuple-element.22) | copy-start | bytes 9437188
  314.1 3.6 %copy-start.2 = (bf16[2,256,1024]{2,1,0:T(8,128)(2,1)S(1)}, bf16[2,256,1024]{2,1,0:T(8,128)(2,1)}, u32[]{:S(2)}) copy-start(bf16[2,256,1024]{2,1,0:T(8,128)(2,1)} %get-tuple-element.23) | copy-start | bytes 3145732
  314.1 5.8 %copy-start.4 = (bf16[1024,256]{1,0:T(8,128)(2,1)S(1)}, bf16[1024,256]{1,0:T(8,128)(2,1)}, u32[]{:S(2)}) copy-start(bf16[1024,256]{1,0:T(8,128)(2,1)} %get-tuple-element.101) | copy-start | bytes 1572868
  317.7 3.0 copy-start.3
